TPU v7x, 512 devices: a whole 4x8x8 slice. The times are simulated.
512 devices in a mesh: ctx: 64 (over x, y, core), head: 8 (over z).
Axes of the slice: x: 4, y: 8, z: 8, core: 2. Of those that a mesh axis runs over, the one named last changes fastest.
Arguments:
- prefill_query: bfloat16 [32768, 32, 128], P('ctx', 'head'), may hold values from -6 to 6
- prefill_key: bfloat16 [32768, 32, 128], P('ctx', 'head'), may hold values from -0.5 to 0.5
- prefill_value: bfloat16 [32768, 32, 128], P('ctx', 'head'), may hold values from -60 to 60
- log_decay: float32 [32768, 32], P('ctx', 'head'), may hold values from -1 to 0
- lengths: int32 [4], replicated, may hold values from 1 to 24576, as said below
- owner: int32 [4], replicated, may hold values from 0 to 127, as said below
- decode_state: float32 [128, 32, 128, 128], P('ctx', 'head'), may hold values from -20 to 20
- step_query: bfloat16 [8, 128, 32, 128], P(None, 'ctx', 'head'), may hold values from -6 to 6
- step_key: bfloat16 [8, 128, 32, 128], P(None, 'ctx', 'head'), may hold values from -0.5 to 0.5
- step_value: bfloat16 [8, 128, 32, 128], P(None, 'ctx', 'head'), may hold values from -6 to 6
- step_decay: float32 [8, 128, 32], P(None, 'ctx', 'head'), may hold values from -0.7 to -0.01
- soft_query: bfloat16 [8, 128, 64, 128], P(None, 'ctx', 'head'), may hold values from -200 to 200
- cache_keys: bfloat16 [128, 256, 8, 128], P('ctx', None, 'head'), may hold values from -6 to 6
- cache_values: bfloat16 [128, 256, 8, 128], P('ctx', None, 'head'), may hold values from -6 to 6
- new_keys: bfloat16 [8, 128, 8, 128], P(None, 'ctx', 'head'), may hold values from -6 to 6
- new_values: bfloat16 [8, 128, 8, 128], P(None, 'ctx', 'head'), may hold values from -6 to 6
- row_lengths: int32 [128], P('ctx'), may hold values from 2 to 256, as said below
Outputs:
- prefill_out: bfloat16 [32768, 32, 128], P('ctx', 'head')
- decode_out: bfloat16 [8, 128, 32, 128], P(None, 'ctx', 'head')
- soft_out: bfloat16 [8, 128, 64, 128], P(None, 'ctx', 'head')
Inputs may be any that keep to these rules, and one draw needn't show every extreme that they name: lengths sum to 32768; the longest is exactly 24576. `owner`: distinct decode rows, including row 0 and row 127. `row_lengths`: row 0 has all 256 slots live.
All inputs are finite; a program needn't handle non-finite values.
Results may differ from a plain program's by a relative error of at most 0.0059.
Values sent between devices are 32-bit elements; how exact they have to be, the bound alone decides.
No kernel may reach another device: no remote copies, remote signals or barrier semaphores. Data moves between devices by JAX's collectives and lax.ppermute only.
A program may use at most 128 MiB of HBM per device.

v0:
```python
import math

import jax
import jax.numpy as jnp
from jax import lax
from jax.sharding import PartitionSpec as P

precise = lax.Precision.HIGHEST
eps = 1e-06


def carried_in(shard, axis, combine, identity):
    devices, mine = (lax.axis_size(axis), lax.axis_index(axis))
    everything = jax.tree.map(lambda part: lax.all_gather(part, axis), shard)
    start = jax.tree.map(
        lambda part, zero: jnp.broadcast_to(jnp.asarray(zero, part.dtype), part.shape),
        shard,
        identity,
    )

    def hop(k, before):
        reached = k < mine
        new = combine(before, jax.tree.map(lambda part: part[k], everything))
        return jax.tree.map(lambda a, b: jnp.where(reached, a, b), new, before)

    return lax.fori_loop(0, devices, hop, start)


def prompt_of(prompt_ends, positions):
    return jnp.sum((positions[:, None] >= prompt_ends[None, :]).astype(jnp.int32), axis=1)


def head_block(pieces, visible):
    queries, key_rows, value_rows, running = pieces
    scores = jnp.dot(queries, key_rows.T, preferred_element_type=jnp.float32)
    decay_grid = jnp.exp(jnp.where(visible, running[:, None] - running[None, :], 0.0))
    weights = jnp.where(visible, scores * decay_grid, 0.0).astype(jnp.bfloat16)
    return jnp.dot(weights, value_rows, preferred_element_type=jnp.float32)


def block_pass(queries, key_rows, value_rows, running, segment, seg_prev, carried):
    block_size = segment.shape[0]
    offsets = jnp.arange(block_size)
    visible = (offsets[:, None] >= offsets[None, :]) & (segment[:, None] == segment[None, :])
    intra = lax.map(
        lambda pieces: head_block(pieces, visible),
        (
            jnp.moveaxis(queries, 1, 0),
            jnp.moveaxis(key_rows, 1, 0),
            jnp.moveaxis(value_rows, 1, 0),
            jnp.moveaxis(running, 1, 0),
        ),
    )
    intra = jnp.moveaxis(intra, 0, 1)
    carry_gate = (segment == seg_prev).astype(jnp.float32)[:, None] * jnp.exp(running)
    carried_term = jnp.einsum(
        "thd,hde->the", queries.astype(jnp.float32), carried, precision=precise
    )
    return intra + carried_term * carry_gate[:, :, None]


def last_summary(key_rows, value_rows, log_decay, running, segment):
    last_prompt = segment[-1]
    inside = (segment == last_prompt)[:, None]
    weight = jnp.where(inside, jnp.exp(jnp.where(inside, running[-1][None, :] - running, 0.0)), 0.0)
    summary = jnp.einsum(
        "thd,the->hde",
        key_rows.astype(jnp.float32) * weight[:, :, None],
        value_rows.astype(jnp.float32),
        precision=precise,
    )
    decay_total = jnp.sum(jnp.where(inside, log_decay, 0.0), axis=0)
    return (decay_total, summary)


def end_states(key_rows, value_rows, running, segment, seg_prev, carried, prompt_ends, block_start):
    block_size = segment.shape[0]
    positions = block_start + jnp.arange(block_size, dtype=jnp.int32)
    key_float = key_rows.astype(jnp.float32)
    value_float = value_rows.astype(jnp.float32)
    collected = []
    for prompt_id in range(prompt_ends.shape[0]):
        last_pos = prompt_ends[prompt_id] - 1
        ends_here = (last_pos >= block_start) & (last_pos < block_start + block_size)
        at_end = (positions == last_pos).astype(jnp.float32)
        running_end = jnp.dot(at_end, running, precision=precise)
        inside = (segment == prompt_id)[:, None] & ends_here
        weight = jnp.where(
            inside, jnp.exp(jnp.where(inside, running_end[None, :] - running, 0.0)), 0.0
        )
        summary = jnp.einsum(
            "thd,the->hde", key_float * weight[:, :, None], value_float, precision=precise
        )
        lead_term = jnp.where(ends_here & (seg_prev == prompt_id), jnp.exp(running_end), 0.0)
        collected.append(summary + lead_term[:, None, None] * carried)
    return jnp.stack(collected)


def combine_states(earlier, later):
    early_sum, early_state, early_flag = earlier
    late_sum, late_state, late_flag = later
    joined = jnp.exp(late_sum)[:, None, None] * early_state + late_state
    restarted = late_flag[0] > 0
    return (
        jnp.where(restarted, late_sum, early_sum + late_sum),
        jnp.where(restarted, late_state, joined),
        jnp.maximum(early_flag, late_flag),
    )


def run_steps(state, query_steps, key_steps, value_steps, decay_steps):
    step_reads = []
    for step_id in range(query_steps.shape[0]):
        outer_term = jnp.einsum(
            "rhd,rhe->rhde",
            key_steps[step_id].astype(jnp.float32),
            value_steps[step_id].astype(jnp.float32),
            precision=precise,
        )
        state = jnp.exp(decay_steps[step_id])[:, :, None, None] * state + outer_term
        step_reads.append(
            jnp.einsum(
                "rhd,rhde->rhe", query_steps[step_id].astype(jnp.float32), state, precision=precise
            )
        )
    return jnp.stack(step_reads)


def attend(query, cache_keys, cache_values, new_keys, new_values, row_lengths):
    step_count, row_count, head_count, head_width = query.shape
    groups = cache_keys.shape[2]
    grouped = query.reshape(step_count, row_count, groups, head_count // groups, head_width)
    inv_root = 1.0 / math.sqrt(head_width)
    cached_scores = (
        jnp.einsum("srkgd,rckd->srkgc", grouped, cache_keys, preferred_element_type=jnp.float32)
        * inv_root
    )
    fresh_scores = (
        jnp.einsum("srkgd,jrkd->srkgj", grouped, new_keys, preferred_element_type=jnp.float32)
        * inv_root
    )
    slot_ids = jnp.arange(cache_keys.shape[1], dtype=jnp.int32)
    live_mask = (slot_ids[None, :] < row_lengths[:, None])[None, :, None, None, :]
    step_ids = jnp.arange(step_count)
    seen_mask = (step_ids[None, :] <= step_ids[:, None])[:, None, None, None, :]
    cached_scores = jnp.where(live_mask, cached_scores, -jnp.inf)
    fresh_scores = jnp.where(seen_mask, fresh_scores, -jnp.inf)
    row_top = jnp.maximum(jnp.max(cached_scores, axis=-1), jnp.max(fresh_scores, axis=-1))[
        ..., None
    ]
    cached_exp = jnp.exp(cached_scores - row_top)
    fresh_exp = jnp.exp(fresh_scores - row_top)
    normalizer = (jnp.sum(cached_exp, axis=-1) + jnp.sum(fresh_exp, axis=-1))[..., None]
    cached_probs = (cached_exp / normalizer).astype(jnp.bfloat16)
    fresh_probs = (fresh_exp / normalizer).astype(jnp.bfloat16)
    mixed = jnp.einsum(
        "srkgc,rckd->srkgd", cached_probs, cache_values, preferred_element_type=jnp.float32
    )
    mixed = mixed + jnp.einsum(
        "srkgj,jrkd->srkgd", fresh_probs, new_values, preferred_element_type=jnp.float32
    )
    return mixed.reshape(step_count, row_count, head_count, head_width).astype(jnp.bfloat16)


def body(
    prefill_query,
    prefill_key,
    prefill_value,
    log_decay,
    lengths,
    owner,
    decode_state,
    step_query,
    step_key,
    step_value,
    step_decay,
    soft_query,
    cache_keys,
    cache_values,
    new_keys,
    new_values,
    row_lengths,
):
    block_size = prefill_query.shape[0]
    head_count = prefill_query.shape[1]
    head_width = prefill_query.shape[2]
    all_heads = head_count * lax.axis_size("head")
    device_index = lax.axis_index("ctx")
    block_start = device_index * block_size
    prompt_ends = jnp.cumsum(lengths)
    prompt_starts = prompt_ends - lengths
    positions = block_start + jnp.arange(block_size, dtype=jnp.int32)
    segment = prompt_of(prompt_ends, positions)
    seg_prev = jnp.where(block_start > 0, prompt_of(prompt_ends, (block_start - 1)[None])[0], -1)
    running = jnp.cumsum(log_decay, axis=0)
    decay_total, summary = last_summary(prefill_key, prefill_value, log_decay, running, segment)
    restart = jnp.any((prompt_starts >= block_start) & (prompt_starts < block_start + block_size))
    restart = restart.astype(jnp.float32)[None]
    identity = (
        jnp.zeros((head_count,), jnp.float32),
        jnp.zeros((head_count, head_width, head_width), jnp.float32),
        jnp.zeros((1,), jnp.float32),
    )
    scanned = carried_in((decay_total, summary, restart), "ctx", combine_states, identity)
    carried = scanned[1]
    mixed = block_pass(
        prefill_query, prefill_key, prefill_value, running, segment, seg_prev, carried
    )
    square_sum = lax.psum(jnp.sum(mixed * mixed, axis=(1, 2)), "head")
    prefill_out = (
        mixed * lax.rsqrt(square_sum / (all_heads * head_width) + eps)[:, None, None]
    ).astype(jnp.bfloat16)
    row_count = decode_state.shape[0]
    row_ids = device_index * row_count + jnp.arange(row_count, dtype=jnp.int32)
    owner_pick = (owner[None, :] == row_ids[:, None]).astype(jnp.float32)
    owned = jnp.sum(owner_pick, axis=1)
    parts = end_states(
        prefill_key, prefill_value, running, segment, seg_prev, carried, prompt_ends, block_start
    )
    handed = lax.psum(parts, "ctx")
    state = jnp.einsum("rp,phde->rhde", owner_pick, handed, precision=precise)
    state = state + (1.0 - owned)[:, None, None, None] * decode_state
    read_steps = run_steps(state, step_query, step_key, step_value, step_decay)
    step_squares = lax.psum(jnp.sum(read_steps * read_steps, axis=(2, 3)), "head")
    decode_out = (
        read_steps * lax.rsqrt(step_squares / (all_heads * head_width) + eps)[:, :, None, None]
    ).astype(jnp.bfloat16)
    soft_out = attend(soft_query, cache_keys, cache_values, new_keys, new_values, row_lengths)
    return (prefill_out, decode_out, soft_out)


def solution(mesh):
    placed = (
        P("ctx", "head", None),
        P("ctx", "head", None),
        P("ctx", "head", None),
        P("ctx", "head"),
        P(),
        P(),
        P("ctx", "head", None, None),
        P(None, "ctx", "head", None),
        P(None, "ctx", "head", None),
        P(None, "ctx", "head", None),
        P(None, "ctx", "head"),
        P(None, "ctx", "head", None),
        P("ctx", None, "head", None),
        P("ctx", None, "head", None),
        P(None, "ctx", "head", None),
        P(None, "ctx", "head", None),
        P("ctx"),
    )
    return jax.shard_map(
        body,
        mesh=mesh,
        in_specs=placed,
        out_specs=(
            P("ctx", "head", None),
            P(None, "ctx", "head", None),
            P(None, "ctx", "head", None),
        ),
        check_vma=False,
    )
```

profile of v0, /device:TPU:6, one launch (start us, length us, event | category | flops | bytes accessed | tf_op | source)
XLA Modules:
  0.0 708.1 jit_solution(3241351327562201482)
XLA Ops:
  23.1 6.8 convert_multiply_fusion.3
  29.8 2.7 fusion.54
  32.7 1.9 copy.405
  34.6 1.9 copy.407
  41.4 109.9 %all-reduce.2 = (f32[64]{0:T(128)}, f32[256]{0:T(256)S(1)}) all-reduce(f32[64]{0:T(128)S(1)} %dynamic-update-slice, f32[256]{0:T(256)S(1)} %dynamic-update-slice.1), channel_id=1, replica_groups=mesh['ctx'=64,'head'=8] {'ctx'}, use_global_device_ids=true, to_apply=%add | all-reduce | flops 320 | bytes 2560
  154.3 1.9 copy.406
  162.1 1.9 slice_exponential_fusion.6
  166.6 9.5 %while.25 = (s32[]{:T(128)}, f32[4,512,128]{1,2,0:T(8,128)}, bf16[4,512,128]{2,1,0:T(8,128)(2,1)}, bf16[4,512,128]{2,1,0:T(8,128)(2,1)}, f32[4,512]{1,0:T(4,128)...) while((s32[]{:T(128)}, f32[4,512,128]{1,2,0:T(8,128)}, ...), condition=%wide.region_5.6_spmd.clone, body=%wide.region_4.5_spmd.clone.sunk | while | flops 136314880 | bytes 669785 | solution.py:45
  166.6 2.4 fusion.131
  169.0 2.3 fusion.131
  171.4 2.4 fusion.131
  173.7 2.4 fusion.131
  176.1 271.8 %while.26 = (s32[]{:T(128)}, f32[4,128,128]{2,1,0:T(8,128)S(1)}, s32[]{:T(128)}, f32[64,1]{0,1:T(1,128)}, f32[64,4,128,128]{3,2,1,0:T(8,128)}, /*index=5*/f32[64,4]{1,0:T(8,128)}, s32[]{:T(128)}, s32[]{:T(128)}) while((s32[]{:T(128)}, f32[4,128,128]{2,1,0:T(8,128)S(1)}, s32[]{:T(128)}, f32[64,1]{0,1:T(1,128)}, ...), condition=%wide.region_9.10_spmd.clone, body=%wide.region_8.9_spmd.clone.sunk | while | flops 327685 | bytes 786603 | solution.py:26
  178.7 1.7 fusion.134
  182.9 1.7 fusion.134
  195.6 1.7 fusion.134
  199.9 1.7 fusion.134
  204.1 1.7 fusion.134
  447.9 2.3 fusion.39
  450.1 2.3 fusion.40
  485.8 2.5 multiply_reduce_fusion
  488.3 181.9 %all-reduce.6.cloned.1.call-done = f32[4,4,128,128]{3,2,1,0:T(8,128)} async-done(((f32[4,4,128,128]{3,2,1,0:T(8,128)}), f32[4,4,128,128]{3,2,1,0:T(8,128)}) %all-reduce.6.cloned.1.call-update) | async-done | bytes 1048592 | tf_op jit(solution)/shard_map/psum | solution.py:220
  670.2 7.7 %multiply_add_fusion = (f32[2,4,128,128]{3,0,2,1:T(2,128)S(1)}, f32[2,4,128,128]{3,0,2,1:T(2,128)S(1)}, f32[2,4,128,128]{3,0,2,1:T(2,128)S(1)}, f32[2,4,128,128]...) fusion(f32[2,4,128]{2,0,1:T(2,128)} %copy.228, ...), kind=kOutput, calls=%fused_computation.94 | convolution fusion | flops 9699336 | bytes 5832992 | tf_op jit(solution)/shard_map/rp,phde->rhde/dot_general | solution.py:221
  681.0 18.3 %all-reduce.3 = (f32[512]{0:T(512)S(1)}, f32[8,2]{1,0:T(8,128)S(1)}) all-reduce(f32[512]{0:T(512)S(1)} %copy-done.11, f32[8,2]{1,0:T(8,128)S(1)} %multiply_reduce_fusion.1), channel_id=1, replica_groups=mesh['ctx'=64,'head'=8] {'head'}, use_global_device_ids=true, to_apply=%region_12.13 | all-reduce | flops 528 | bytes 4224 | tf_op jit(solution)/shard_map/psum | solution.py:209
  (329 shorter events, 327.9 us)
Async XLA Ops:
  7.2 150.8 %copy-start = (bf16[2,256,1,128]{3,1,2,0:T(8,128)(2,1)S(1)}, bf16[2,256,1,128]{3,1,2,0:T(8,128)(2,1)}, u32[]{:S(2)}) copy-start(bf16[2,256,1,128]{3,1,2,0:T(8,128)(2,1)} %param.33) | copy-start | bytes 393220
  7.2 168.9 %all-gather.4.cloned.1.call-start = ((), (), s32[]{:S(2)}) async-start(), calls=%async_computation.1 | async-start | bytes 17039360 | tf_op jit(solution)/shard_map/all_gather | solution.py:14
  12.2 8.7 %copy-start.12 = (s32[512]{0:T(512)}, s32[512]{0:T(512)S(1)}, u32[]{:S(2)}) copy-start(s32[512]{0:T(512)S(1)} %convert_reduce_fusion) | copy-start | bytes 6148
  23.1 424.8 %copy-start.1 = (bf16[512,4,128]{2,1,0:T(4,128)(2,1)S(1)}, bf16[512,4,128]{2,1,0:T(4,128)(2,1)}, u32[]{:S(2)}) copy-start(bf16[512,4,128]{2,1,0:T(4,128)(2,1)} %param.23) | copy-start | bytes 1572868
  32.6 637.6 %all-reduce.6.cloned.1.call-start = ((), (), s32[]{:S(2)}) async-start(), calls=%async_computation | async-start | bytes 2097152 | tf_op jit(solution)/shard_map/psum | solution.py:220
  159.3 7.4 %copy-start.13 = (s32[2]{0:T(128)}, s32[2]{0:T(128)S(1)}, u32[]{:S(2)}) copy-start(s32[2]{0:T(128)S(1)} %iota_add_fusion.1) | copy-start | bytes 28
  163.9 321.9 %copy-start.2 = (bf16[512,4,128]{2,1,0:T(4,128)(2,1)S(1)}, bf16[512,4,128]{2,1,0:T(4,128)(2,1)}, u32[]{:S(2)}) copy-start(bf16[512,4,128]{2,1,0:T(4,128)(2,1)} %param.21) | copy-start | bytes 1572868
  176.1 285.0 %copy-start.10 = (f32[2,4,128]{2,1,0:T(4,128)S(1)}, f32[2,4,128]{2,1,0:T(4,128)}, u32[]{:S(2)}) copy-start(f32[2,4,128]{2,1,0:T(4,128)} %get-tuple-element.258) | copy-start | bytes 12292
  176.1 309.7 %copy-start.3 = (f32[512,4]{0,1:T(4,128)S(1)}, f32[512,4]{0,1:T(4,128)}, u32[]{:S(2)}) copy-start(f32[512,4]{0,1:T(4,128)} %get-tuple-element.271) | copy-start | bytes 24580
  488.3 189.6 %copy-start.9 = (bf16[2,4,128,1]{2,1,0,3:T(4,128)(2,1)S(1)}, bf16[2,4,128,1]{2,1,0,3:T(4,128)(2,1)}, u32[]{:S(2)}) copy-start(bf16[2,4,128,1]{2,1,0,3:T(4,128)(2,1)} %get-tuple-element.249) | copy-start | bytes 6148
  488.3 190.0 %copy-start.8 = (bf16[2,4,128,1]{2,1,0,3:T(4,128)(2,1)S(1)}, bf16[2,4,128,1]{2,1,0,3:T(4,128)(2,1)}, u32[]{:S(2)}) copy-start(bf16[2,4,128,1]{2,1,0,3:T(4,128)(2,1)} %get-tuple-element.248) | copy-start | bytes 6148
  488.3 190.3 %copy-start.7 = (bf16[2,4,128,1]{2,1,0,3:T(4,128)(2,1)S(1)}, bf16[2,4,128,1]{2,1,0,3:T(4,128)(2,1)}, u32[]{:S(2)}) copy-start(bf16[2,4,128,1]{2,1,0,3:T(4,128)(2,1)} %get-tuple-element.247) | copy-start | bytes 6148
  670.2 8.8 %copy-start.6 = (bf16[2,4,128,1]{2,1,0,3:T(4,128)(2,1)S(1)}, bf16[2,4,128,1]{2,1,0,3:T(4,128)(2,1)}, u32[]{:S(2)}) copy-start(bf16[2,4,128,1]{2,1,0,3:T(4,128)(2,1)} %get-tuple-element.246) | copy-start | bytes 6148
  670.2 9.2 %copy-start.5 = (bf16[2,4,128,1]{2,1,0,3:T(4,128)(2,1)S(1)}, bf16[2,4,128,1]{2,1,0,3:T(4,128)(2,1)}, u32[]{:S(2)}) copy-start(bf16[2,4,128,1]{2,1,0,3:T(4,128)(2,1)} %get-tuple-element.245) | copy-start | bytes 6148
  670.2 9.6 %copy-start.4 = (bf16[2,4,128,1]{2,1,0,3:T(4,128)(2,1)S(1)}, bf16[2,4,128,1]{2,1,0,3:T(4,128)(2,1)}, u32[]{:S(2)}) copy-start(bf16[2,4,128,1]{2,1,0,3:T(4,128)(2,1)} %get-tuple-element.244) | copy-start | bytes 6148
  670.2 10.8 %copy-start.11 = (f32[512]{0:T(512)S(1)}, f32[512]{0:T(512)}, u32[]{:S(2)}) copy-start(f32[512]{0:T(512)} %get-tuple-element.294) | copy-start | bytes 6148
Sparse Core Ops, SparseCore 0:
  32.7 108.0 all-gather.3
  457.0 213.1 all-reduce.5
where the time goes:
time: 716 us; the launch traced here: 708 us
  other arithmetic  214 us (30%)
  waiting for transfers between devices  182 us (25%)
  blocking collectives  128 us (18%)
  local copies, waits for them, and re-layouts  123 us (17%)
  matrix products  40.6 us (6%)
  between operations  19.1 us (3%)
    psum x1, waiting for transfers between devices, body(): handed = lax.psum(parts, 'ctx')  182 us
    unnamed x1, blocking collectives  110 us
    select_n x64, other arithmetic, hop(): return jax.tree.map(lambda a, b: jnp.where(reached, a, b), new, before)  108 us
    gt x64, other arithmetic, combine_states(): restarted = late_flag[0] > 0  84.8 us
    exp x64, local copies, waits for them, and re-layouts, combine_states(): joined = jnp.exp(late_sum)[:, None, None] * early_state + late_state  77.3 us
    psum x1, blocking collectives, body(): square_sum = lax.psum(jnp.sum(mixed * mixed, axis=(1, 2)), 'head')  18.3 us
    another operation x16, local copies, waits for them, and re-layouts  16.1 us
  transfers between devices with their start and end apart: 2, of which 1 were waited for; matrix products, arithmetic and copies ran while one was open for 9% of the time, Pallas kernels for 0%

commit v1 on v0

v1 whole, which is shorter than its diff:
```python
import functools
import math

import jax
import jax.numpy as jnp
from jax import lax
from jax.experimental import pallas as pl
from jax.experimental.pallas import tpu as pltpu
from jax.sharding import PartitionSpec as P

f32 = jnp.float32
bf16 = jnp.bfloat16
eps = 1e-06
HD = 128
HALF = HD // 2
ROW_END = 8
ROW_QUERY = 24
ROW_DECAY = 26
ROWS_OUT = 32
ROWS_BACK = 16
NT = (((1,), (1,)), ((), ()))
TN = (((0,), (0,)), ((), ()))
NN = (((1,), (0,)), ((), ()))


def mm(a, b, dims=NN):
    return lax.dot_general(a, b, dims, preferred_element_type=f32)


def iota(shape, dim):
    return lax.broadcasted_iota(jnp.int32, shape, dim)


def two(x):
    high = x.astype(bf16)
    return high, (x - high.astype(f32)).astype(bf16)


def three(x):
    high = x.astype(bf16)
    rest = x - high.astype(f32)
    mid = rest.astype(bf16)
    return high, mid, (rest - mid.astype(f32)).astype(bf16)


def prompt_bounds(lengths):
    ends, total = [], jnp.int32(0)
    starts = []
    for p in range(lengths.shape[0]):
        starts.append(total)
        total = total + lengths[p]
        ends.append(total)
    return starts, ends


def segment_of(positions, ends):
    segment = jnp.zeros(positions.shape, jnp.int32)
    for end in ends:
        segment = segment + (positions >= end).astype(jnp.int32)
    return segment


def scalar_segment(position, ends):
    segment = jnp.int32(0)
    for end in ends:
        segment = segment + (position >= end).astype(jnp.int32)
    return segment


def swap_halves(first, second):
    left = iota((1, HD), 1) < HALF
    shape = first.shape
    rolled_first = pltpu.roll(first.reshape(-1, HD), HALF, 1).reshape(shape)
    rolled_second = pltpu.roll(second.reshape(-1, HD), HALF, 1).reshape(shape)
    left = left.reshape((1,) * (len(shape) - 1) + (HD,))
    return jnp.where(left, first, rolled_second), jnp.where(left, rolled_first, second)


def cut(matrix):
    split = matrix.reshape(8, 2, 8, HD)
    low, high = swap_halves(split[:, 0], split[:, 1])
    return jnp.stack([low, high], axis=1).reshape(16, 8, HD)


def uncut(chunks):
    split = chunks.reshape(8, 2, 8, HD)
    low, high = swap_halves(split[:, 0], split[:, 1])
    return jnp.stack([low, high], axis=1).reshape(HD, HD)


def end_slot(slot, ends, block_start, block):
    prompt, offset = jnp.int32(-1), jnp.int32(-1)
    for p in range(len(ends)):
        if p % 2 != slot:
            continue
        local = ends[p] - 1 - block_start
        inside = (local >= 0) & (local < block) & (lax.rem(ends[p], block) != 0)
        prompt = jnp.where(inside, p, prompt)
        offset = jnp.where(inside, local, offset)
    return prompt, offset


def summary_kernel(lengths, decay, key, value, step_query, out, running_out):
    heads, block = decay.shape
    block_start = lax.axis_index("ctx") * block
    _, ends = prompt_bounds(lengths)
    place = iota((1, block), 1)
    segment = segment_of(place + block_start, ends)
    last = scalar_segment(block_start + block - 1, ends)
    prompt_a, offset_a = end_slot(0, ends, block_start, block)
    prompt_b, offset_b = end_slot(1, ends, block_start, block)

    parts = jnp.concatenate(three(decay[...]), axis=0)
    upto = (iota((block, block), 0) <= iota((block, block), 1)).astype(f32).astype(bf16)
    sums = mm(parts, upto)
    running = sums[:heads] + sums[heads : 2 * heads] + sums[2 * heads :]
    running_out[...] = jnp.concatenate([running, running], axis=0)

    row = iota((8, block), 0)
    spot = iota((8, block), 1)
    span = jnp.where(
        row == 0,
        (jnp.broadcast_to(segment, (8, block)) == last).astype(f32),
        jnp.where(
            row == 1,
            (spot <= offset_a).astype(f32),
            jnp.where(row == 2, (spot <= offset_b).astype(f32), 0.0),
        ),
    )
    spans = mm(span.astype(bf16), parts, NT)
    totals = spans[:, :heads] + spans[:, heads : 2 * heads] + spans[:, 2 * heads :]
    totals = jnp.concatenate([totals, jnp.zeros((8, HD - heads), f32)], axis=1)
    out[:, ROW_QUERY:ROWS_OUT, :] = jnp.zeros((out.shape[0], ROWS_OUT - ROW_QUERY, HD), f32)
    out[:, ROW_DECAY : ROW_DECAY + 3, :] = jnp.broadcast_to(
        totals[None, 0:3], (out.shape[0], 3, HD)
    )

    def weight(prompt, offset):
        inside = segment == prompt
        at = jnp.sum(jnp.where(place == offset, running, 0.0), axis=1, keepdims=True)
        return jnp.where(inside, jnp.exp(jnp.where(inside, at - running, 0.0)), 0.0)

    weights = jnp.concatenate(
        [
            weight(last, jnp.int32(block - 1)),
            weight(prompt_a, offset_a),
            weight(prompt_b, offset_b),
            jnp.zeros((4, block), f32),
        ],
        axis=0,
    )
    columns = weights.T

    keys = jnp.swapaxes(key[...], 0, 1)
    values = jnp.swapaxes(value[...], 0, 1)
    for h in range(heads):
        value_h = values[h].astype(f32)
        right = []
        for k in range(3):
            c = k * heads + h
            right.extend(two(value_h * columns[:, c : c + 1]))
        product = mm(keys[h], jnp.concatenate(right, axis=1), TN)
        for k in range(3):
            low = 2 * k * HD
            state = product[:, low : low + HD] + product[:, low + HD : low + 2 * HD]
            out[16 * h : 16 * h + 16, 8 * k : 8 * k + 8, :] = cut(state)

    steps, rows = step_query.shape[0], step_query.shape[1]
    flat = step_query[...].astype(f32).reshape(steps * rows * heads, HD).astype(bf16)
    d_at, lane = iota((HD, 8 * HD), 0), iota((HD, 8 * HD), 1)
    pick = (d_at == (lane // HD) * 16 + lane % 16).astype(f32).astype(bf16)
    spread = mm(flat, pick).reshape(steps, rows * heads, 8 * HD)
    step_at = iota((steps, 1, 8 * HD), 0)
    lane3 = iota((steps, 1, 8 * HD), 2)
    spread = jnp.sum(jnp.where((lane3 % HD) // 16 == step_at, spread, 0.0), axis=0)
    for r in range(rows):
        for h in range(heads):
            for d in range(8):
                piece = spread[r * heads + h : r * heads + h + 1, d * HD : (d + 1) * HD]
                for e in range(2):
                    j = 16 * h + 2 * d + e
                    out[j, ROW_QUERY + r : ROW_QUERY + r + 1, :] = piece


def local_kernel(
    lengths,
    owner,
    row_lengths,
    running_in,
    query,
    key,
    value,
    decode_state,
    step_query,
    step_key,
    step_value,
    step_decay,
    soft_query,
    cache_keys,
    cache_values,
    new_keys,
    new_values,
    intra_out,
    query_out,
    gate_out,
    base_out,
    coef_out,
    soft_out,
):
    block, heads, _ = query.shape
    device = lax.axis_index("ctx")
    block_start = device * block
    _, ends = prompt_bounds(lengths)
    running = running_in[...]
    columns = running.T
    place_row = iota((1, block), 1) + block_start
    place_col = iota((block, 1), 0) + block_start
    segment_row = segment_of(place_row, ends)
    segment_col = segment_of(place_col, ends)
    before = jnp.where(block_start > 0, scalar_segment(block_start - 1, ends), -1)
    gate_out[...] = jnp.where(segment_col == before, jnp.exp(columns), 0.0)

    queries = jnp.swapaxes(query[...], 0, 1)
    keys = jnp.swapaxes(key[...], 0, 1)
    values = jnp.swapaxes(value[...], 0, 1)
    query_out[...] = queries
    half = block // 2
    tiles = ((0, 0), (1, 0), (1, 1))
    masks = {}
    for a, b in tiles:
        rows = slice(a * half, (a + 1) * half)
        cols = slice(b * half, (b + 1) * half)
        seen = segment_col[rows] == segment_row[:, cols]
        if a == b:
            seen = seen & (place_col[rows] >= place_row[:, cols])
        masks[a, b] = jnp.where(seen, 0.0, -1e30)
    for h in range(heads):
        mixed = [None, None]
        for a, b in tiles:
            rows = slice(a * half, (a + 1) * half)
            cols = slice(b * half, (b + 1) * half)
            scores = mm(queries[h][rows], keys[h][cols], NT)
            gap = columns[rows, h : h + 1] - running[h : h + 1, cols]
            weights = (scores * jnp.exp(gap + masks[a, b])).astype(bf16)
            term = mm(weights, values[h][cols])
            mixed[a] = term if mixed[a] is None else mixed[a] + term
        intra_out[h, :half, :] = mixed[0]
        intra_out[h, half:, :] = mixed[1]

    steps, rows_n = step_query.shape[0], step_query.shape[1]

    def by_head(ref):
        whole = ref[...].astype(f32).reshape(steps, rows_n * heads, HD)
        return jnp.swapaxes(whole, 0, 1)

    sq, sk, sv = by_head(step_query), by_head(step_key), by_head(step_value)
    decays = step_decay[...].reshape(rows_n * heads, steps)
    upto = (iota((steps, steps), 0) <= iota((steps, steps), 1)).astype(f32)
    cum_row = lax.dot_general(
        decays, upto, NN, precision=lax.Precision.HIGHEST, preferred_element_type=f32
    )
    cum_col = cum_row.T
    causal = iota((steps, steps), 0) >= iota((steps, steps), 1)
    for r in range(rows_n):
        owned = jnp.int32(0)
        for p in range(len(ends)):
            owned = owned + (owner[p] == device * rows_n + r).astype(jnp.int32)
        owned = jnp.where(owned > 0, 1.0, 0.0)
        for h in range(heads):
            n = r * heads + h
            cum = cum_col[:, n : n + 1]
            gap = jnp.where(causal, cum - cum_row[n : n + 1, :], 0.0)
            inner = mm(sq[n].astype(bf16), sk[n].astype(bf16), NT)
            inner = jnp.where(causal, inner * jnp.exp(gap), 0.0)
            fresh = lax.dot_general(
                inner, sv[n], NN, precision=lax.Precision.HIGHEST, preferred_element_type=f32
            )
            high, low = two(decode_state[r, h])
            read = mm(sq[n].astype(bf16), jnp.concatenate([high, low], axis=1))
            grown = jnp.exp(cum)
            read = (read[:, :HD] + read[:, HD:]) * grown
            base_out[n] = fresh + jnp.where(owned > 0.5, 0.0, read)
            coef_out[n] = jnp.broadcast_to(grown * owned, (steps, HD))

    fresh_keys = jnp.swapaxes(new_keys[...].astype(f32), 0, 1)
    fresh_values = jnp.swapaxes(new_values[...].astype(f32), 0, 1)
    group = soft_query.shape[2]
    cache = cache_keys.shape[1]
    scale = 1.0 / math.sqrt(HD)
    whole = soft_query[...].astype(f32)
    for r in range(rows_n):
        rows_q = whole[:, r].reshape(steps * group, HD).astype(bf16)
        cached = mm(rows_q, cache_keys[r], NT) * scale
        recent = mm(rows_q, fresh_keys[r].astype(bf16), NT) * scale
        slot = iota((steps * group, cache), 1)
        cached = jnp.where(slot < row_lengths[r], cached, -jnp.inf)
        step_of = iota((steps * group, steps), 0) // group
        recent = jnp.where(iota((steps * group, steps), 1) <= step_of, recent, -jnp.inf)
        top = jnp.maximum(
            jnp.max(cached, axis=1, keepdims=True), jnp.max(recent, axis=1, keepdims=True)
        )
        cached = jnp.exp(cached - top)
        recent = jnp.exp(recent - top)
        total = jnp.sum(cached, axis=1, keepdims=True) + jnp.sum(recent, axis=1, keepdims=True)
        cached = (cached / total).astype(bf16)
        recent = (recent / total).astype(bf16)
        mixed = mm(cached, cache_values[r]) + mm(recent, fresh_values[r].astype(bf16))
        soft_out[:, r, :, :] = mixed.reshape(steps, group, HD).astype(bf16)


def scan_kernel(lengths, owner, got, out, carried):
    blocks = got.shape[0]
    block = lengths_block(blocks)
    device = lax.axis_index("ctx")
    head = device // 16
    starts, ends = prompt_bounds(lengths)
    padded = carried.shape[0]

    decays = got[:, ROW_DECAY, :]
    decay = jnp.sum(
        jnp.where(iota((blocks, HD), 1) == head, decays, 0.0), axis=1, keepdims=True
    )
    k_at, b_at = iota((blocks, blocks), 0), iota((blocks, blocks), 1)
    later = jnp.concatenate(
        [jnp.where(k_at > b_at, part.astype(f32), 0.0).astype(bf16) for part in three(decay)],
        axis=1,
    )
    earlier = (iota((padded, blocks), 1) < iota((padded, blocks), 0)).astype(f32).astype(bf16)
    gaps = mm(earlier, later)
    gap = gaps[:, :blocks] + gaps[:, blocks : 2 * blocks] + gaps[:, 2 * blocks :]
    to, frm = iota((padded, blocks), 0), iota((padded, blocks), 1)
    linked = frm < to
    for start in starts:
        restart = start // block
        linked = linked & ~((restart > frm) & (restart < to))
    weight = jnp.where(linked, jnp.exp(jnp.where(linked, gap, 0.0)), 0.0)
    weights = jnp.concatenate(two(weight), axis=0)
    for i in range(8):
        high, low = two(got[:, i, :])
        product = mm(weights, jnp.concatenate([high, low], axis=1))
        state = product[:padded, :HD] + product[padded:, :HD] + product[:padded, HD:]
        carried[:, i, :] = state
        out[:, i, :] = state[:blocks]

    out[:, 8:ROWS_BACK, :] = jnp.zeros((blocks, ROWS_BACK - 8, HD), f32)
    rows_n = 2
    for p in range(len(ends)):
        slot = p % 2
        index = ends[p] // block
        source = jnp.minimum(index, blocks - 1)
        partial = (lax.rem(ends[p], block) != 0).astype(f32)
        leads = (starts[p] < index * block).astype(f32)
        run = got[source, ROW_DECAY + 1 + slot : ROW_DECAY + 2 + slot, :]
        run = jnp.sum(jnp.where(iota((1, HD), 1) == head, run, 0.0), axis=1, keepdims=True)
        lead = leads * jnp.exp(run * partial)
        low_row = ROW_END + 8 * slot
        handed = carried[index] * lead + got[source, low_row : low_row + 8, :] * partial
        high, low = two(jnp.concatenate([handed[:, :HALF], handed[:, HALF:]], axis=0))
        right = jnp.concatenate([jnp.concatenate([high, low], axis=1)] * 8, axis=0)
        place = owner[p] // rows_n
        side = lax.rem(owner[p], rows_n)
        pair = got[place, ROW_QUERY : ROW_QUERY + rows_n, :]
        query = jnp.where(side == 0, pair[0:1], pair[1:2])
        steps = 8
        lane = iota((steps, HD), 1)
        query = jnp.where(lane // 16 == iota((steps, HD), 0), query, 0.0).astype(bf16)
        read = mm(query, right)
        read = read[:, :HALF] + read[:, HALF:]
        both = jnp.concatenate([read, read], axis=1)
        old = out[place, 8:ROWS_BACK, :]
        out[place, 8:ROWS_BACK, :] = jnp.where(lane // HALF == side, both, old)


def lengths_block(blocks):
    return 512


def mix_kernel(got, intra, query, gate, base, coef, mixed_out, reads_out, squares_out):
    heads, block, _ = intra.shape
    total = None
    for h in range(heads):
        state = uncut(got[16 * h : 16 * h + 16, 0:8, :])
        high, low = two(state)
        read = mm(query[h], jnp.concatenate([high, low], axis=1))
        mixed = intra[h] + (read[:, :HD] + read[:, HD:]) * gate[:, h : h + 1]
        mixed_out[h] = mixed
        total = mixed * mixed if total is None else total + mixed * mixed
    ones = jnp.ones((8, HD), bf16)
    high, low = two(total)
    squares_out[:, 0, :block] = mm(ones, high, NT) + mm(ones, low, NT)

    rows_n = base.shape[0] // heads
    squares = [None] * rows_n
    for h in range(heads):
        first, second = None, None
        for d in range(8):
            a = got[16 * h + 2 * d, 8:16, :]
            b = got[16 * h + 2 * d + 1, 8:16, :]
            first = a if first is None else first + a
            second = b if second is None else second + b
        for r, handed in enumerate(swap_halves(first, second)):
            n = r * heads + h
            read = base[n] + coef[n] * handed
            reads_out[n] = read
            squares[r] = read * read if squares[r] is None else squares[r] + read * read
    high, low = two(jnp.concatenate(squares, axis=0))
    sums = mm(ones, high, NT) + mm(ones, low, NT)
    squares_out[:, 0, block:] = jnp.concatenate(
        [sums, jnp.zeros((8, HD - sums.shape[1]), f32)], axis=1
    )


def norm_kernel(count, got, mixed, reads, prefill_out, decode_out):
    heads, block, _ = mixed.shape
    parts = jnp.concatenate(three(got[:, 0, :]), axis=0)
    ones = jnp.ones((parts.shape[0], HD), bf16)
    total = mm(parts, ones, TN)
    scale = lax.rsqrt(total / count + eps)
    scaled = jnp.stack([mixed[h] * scale[:block] for h in range(heads)], axis=0)
    prefill_out[...] = jnp.swapaxes(scaled, 0, 1).astype(bf16)
    steps, rows_n = decode_out.shape[0], decode_out.shape[1]
    pieces = []
    for r in range(rows_n):
        low = block + r * steps
        for h in range(heads):
            pieces.append(reads[r * heads + h] * scale[low : low + steps])
    scaled = jnp.swapaxes(jnp.stack(pieces, axis=0), 0, 1)
    decode_out[...] = scaled.reshape(decode_out.shape).astype(bf16)


def call(kernel, name, outs, scalars, arrays, scratch=(), cost=0):
    shapes = [jax.ShapeDtypeStruct(shape, dtype) for shape, dtype in outs]
    specs = [pl.BlockSpec(memory_space=pltpu.SMEM)] * len(scalars)
    specs += [pl.BlockSpec(memory_space=pltpu.VMEM)] * len(arrays)
    return pl.pallas_call(
        kernel,
        name=name,
        out_shape=shapes,
        in_specs=specs,
        out_specs=[pl.BlockSpec(memory_space=pltpu.VMEM)] * len(outs),
        scratch_shapes=list(scratch),
        compiler_params=pltpu.CompilerParams(vmem_limit_bytes=24 * 2**20),
        cost_estimate=pl.CostEstimate(flops=cost, bytes_accessed=4 * 2**20, transcendentals=0),
    )(*scalars, *arrays)


def body(
    prefill_query,
    prefill_key,
    prefill_value,
    log_decay,
    lengths,
    owner,
    decode_state,
    step_query,
    step_key,
    step_value,
    step_decay,
    soft_query,
    cache_keys,
    cache_values,
    new_keys,
    new_values,
    row_lengths,
):
    block, heads, _ = prefill_query.shape
    steps, rows_n = step_query.shape[0], step_query.shape[1]
    blocks = lax.axis_size("ctx")
    planes = lax.axis_size("head")
    pairs = rows_n * heads
    decay_rows = jnp.swapaxes(log_decay, 0, 1)
    outgoing, running = call(
        summary_kernel,
        "summary",
        [((blocks, ROWS_OUT, HD), f32), ((8, block), f32)],
        [lengths],
        [decay_rows, prefill_key, prefill_value, step_query],
    )
    gathered = lax.all_to_all(outgoing, "ctx", 0, 0, tiled=True)
    intra, queries, gate, base, coef, soft_out = call(
        local_kernel,
        "local",
        [
            ((heads, block, HD), f32),
            ((heads, block, HD), bf16),
            ((block, 8), f32),
            ((pairs, steps, HD), f32),
            ((pairs, steps, HD), f32),
            (soft_query.shape, bf16),
        ],
        [lengths, owner, row_lengths],
        [
            running,
            prefill_query,
            prefill_key,
            prefill_value,
            decode_state,
            step_query,
            step_key,
            step_value,
            jnp.transpose(step_decay, (1, 2, 0)),
            soft_query,
            cache_keys.reshape(rows_n, -1, HD),
            cache_values.reshape(rows_n, -1, HD),
            new_keys.reshape(steps, rows_n, HD),
            new_values.reshape(steps, rows_n, HD),
        ],
        cost=2 * 10**9,
    )
    returning = call(
        scan_kernel,
        "scan",
        [((blocks, ROWS_BACK, HD), f32)],
        [lengths, owner],
        [gathered],
        scratch=[pltpu.VMEM((blocks + 8, 8, HD), f32)],
    )[0]
    returned = lax.all_to_all(returning, "ctx", 0, 0, tiled=True)
    mixed, reads, squares = call(
        mix_kernel,
        "mix",
        [
            ((heads, block, HD), f32),
            ((pairs, steps, HD), f32),
            ((planes, 1, block + HD), f32),
        ],
        [],
        [returned, intra, queries, gate, base, coef],
    )
    squares = lax.all_to_all(squares, "head", 0, 0, tiled=True)
    prefill_out, decode_out = call(
        functools.partial(norm_kernel, float(planes * heads * HD)),
        "norm",
        [(prefill_query.shape, bf16), (step_query.shape, bf16)],
        [],
        [squares, mixed, reads],
    )
    return (prefill_out, decode_out, soft_out)


def solution(mesh):
    placed = (
        P("ctx", "head", None),
        P("ctx", "head", None),
        P("ctx", "head", None),
        P("ctx", "head"),
        P(),
        P(),
        P("ctx", "head", None, None),
        P(None, "ctx", "head", None),
        P(None, "ctx", "head", None),
        P(None, "ctx", "head", None),
        P(None, "ctx", "head"),
        P(None, "ctx", "head", None),
        P("ctx", None, "head", None),
        P("ctx", None, "head", None),
        P(None, "ctx", "head", None),
        P(None, "ctx", "head", None),
        P("ctx"),
    )
    return jax.shard_map(
        body,
        mesh=mesh,
        in_specs=placed,
        out_specs=(
            P("ctx", "head", None),
            P(None, "ctx", "head", None),
            P(None, "ctx", "head", None),
        ),
        check_vma=False,
    )
```

time: 716 us -> 94.1 us (0.13)
  other arithmetic: 214 us -> 0 us
  waiting for transfers between devices: 182 us -> 6.09 us
  local copies, waits for them, and re-layouts: 123 us -> 10.1 us
  blocking collectives: 128 us -> 55.2 us
  matrix products: 40.6 us -> 0 us
  between operations: 19.1 us -> 0.79 us
  Pallas kernels: 0 us -> 12.8 us
  starting transfers between devices: 0.08 us -> 8.23 us
    psum x1 -> x0, waiting for transfers between devices: 182 us -> none  [body(): handed = lax.psum(parts, 'ctx')]
    unnamed x1 -> x0, blocking collectives: 110 us -> none
    select_n x65 -> x0, other arithmetic: 110 us -> none  [the longest x64 108 us: hop(): return jax.tree.map(lambda a, b: jnp.where(reached, a, b), new, before)]
    exp x73 -> x0, local copies, waits for them, and re-layouts: 89.9 us -> none  [the longest x64 77.3 us: combine_states(): joined = jnp.exp(late_sum)[:, None, None] * early_state + late_state]
    gt x64 -> x0, other arithmetic: 84.8 us -> none  [combine_states(): restarted = late_flag[0] > 0]
    all_to_all x0 -> x2, blocking collectives: none -> 55.2 us  [the longest x1 37.3 us: body(): gathered = lax.all_to_all(outgoing, 'ctx', 0, 0, tiled=True)]
    dot_general x27 -> x0, matrix products: 40.6 us -> none  [the longest x4 9.45 us: head_block(): return jnp.dot(weights, value_rows, preferred_element_type=jnp.float32)]
    psum x1 -> x0, blocking collectives: 18.3 us -> none  [body(): square_sum = lax.psum(jnp.sum(mixed * mixed, axis=(1, 2)), 'head')]
  transfers between devices with their start and end apart: 2 -> 1, of which waited for: 1 -> 1; matrix products, arithmetic and copies ran while one was open for 9% -> 0% of each run, Pallas kernels for 0% -> 5%
where the time goes in v1:
time: 94.1 us; the launch traced here: 93.2 us
  blocking collectives  55.2 us (59%)
  Pallas kernels  12.8 us (14%)
  local copies, waits for them, and re-layouts  10.1 us (11%)
  starting transfers between devices  8.23 us (9%)
  waiting for transfers between devices  6.09 us (6%)
    all_to_all x1, blocking collectives, body(): gathered = lax.all_to_all(outgoing, 'ctx', 0, 0, tiled=True)  37.3 us
    all_to_all x1, blocking collectives, body(): squares = lax.all_to_all(squares, 'head', 0, 0, tiled=True)  17.9 us
    pallas_call x5, Pallas kernels, call(): pl.pallas_call(kernel, name=name, out_shape=shapes, in_specs=specs, out_s...  12.8 us
    unnamed x44, local copies, waits for them, and re-layouts  10.1 us
    all_to_all x1, starting transfers between devices, body(): returned = lax.all_to_all(returning, 'ctx', 0, 0, tiled=True)  8.23 us
    all_to_all x1, waiting for transfers between devices, body(): returned = lax.all_to_all(returning, 'ctx', 0, 0, tiled=True)  6.09 us
  transfers between devices with their start and end apart: 1, of which 1 were waited for; matrix products, arithmetic and copies ran while one was open for 0% of the time, Pallas kernels for 5%

profile of v1, /device:TPU:6, one launch (start us, length us, event | category | flops | bytes accessed | tf_op | source)
XLA Modules:
  0.0 93.2 jit_solution(9456251851011333928)
XLA Ops:
  0.6 0.6 copy-done.7
  1.3 1.0 %copy-done = bf16[512,4,128]{2,1,0:T(4,128)(2,1)S(1)} copy-done((bf16[512,4,128]{2,1,0:T(4,128)(2,1)S(1)}, bf16[512,4,128]{2,1,0:T(4,128)(2,1)}, u32[]{:S(2)}) %copy-start) | copy-done | bytes 524312
  2.3 1.0 %copy-done.2 = bf16[512,4,128]{2,1,0:T(4,128)(2,1)S(1)} copy-done((bf16[512,4,128]{2,1,0:T(4,128)(2,1)S(1)}, bf16[512,4,128]{2,1,0:T(4,128)(2,1)}, u32[]{:S(2)}) %copy-start.2) | copy-done | bytes 524312
  3.4 0.7 copy-done.4
  4.1 0.7 copy-done.6
  4.8 3.0 %summary.1 = (f32[64,32,128]{2,1,0:T(8,128)S(1)}, f32[8,512]{1,0:T(8,128)S(1)}) custom-call(s32[4]{0:T(128)S(1)} %copy-done.7, f32[4,512]{1,0:T(4,128)S(1)} %bitcast.6, bf16[512,4,128]{2,1,0:T(4,128)(2,1)S(1)} %copy-done, bf16[512,4,128]{2,1,0:T(4,128)(2,1)S(1)} %copy-done.2, bf16[8,2,4,128]{3,2,1,0:T(4,128)(2,1)S(1)} %copy-done.4), custom_call_target="tpu_custom_call" | custom-call | bytes 4194304 | tf_op jit(solution)/shard_map/summary/pallas_call | solution.py:435
  7.8 0.0 copy-start.16
  7.8 0.0 copy-start.8
  7.8 37.3 %all_to_all.15.got = f32[64,32,128]{2,1,0:T(8,128)S(1)} all-to-all(f32[64,32,128]{2,1,0:T(8,128)S(1)} %get-tuple-element.16), channel_id=1, replica_groups=mesh['ctx'=64,'head'=8] {'ctx'}, dimensions={0} | all-to-all | bytes 2097152 | tf_op jit(solution)/shard_map/all_to_all | solution.py:479
  45.1 3.2 %scan.1 = f32[64,16,128]{2,1,0:T(8,128)} custom-call(s32[4]{0:T(128)S(1)} %copy-done.7, s32[4]{0:T(128)S(1)} %copy-done.8, f32[64,32,128]{2,1,0:T(8,128)S(1)} %all_to_all.15.got), custom_call_target="tpu_custom_call" | custom-call | bytes 4194304 | tf_op jit(solution)/shard_map/scan/pallas_call | solution.py:435
  48.3 8.2 %all-to-all-start.1 = ((f32[64,16,128]{2,1,0:T(8,128)}), f32[64,16,128]{2,1,0:T(8,128)S(1)}, u32[]{:S(2)}, u32[]{:S(2)}) async-start(f32[64,16,128]{2,1,0:T(8,128)} %scan.1), calls=%async_computation.1 | async-start | bytes 1048576 | tf_op jit(solution)/shard_map/all_to_all | solution.py:518
  56.6 0.6 copy-done.19
  57.2 0.0 copy-done.18
  57.2 1.0 %copy-done.9 = bf16[512,4,128]{2,1,0:T(4,128)(2,1)S(1)} copy-done((bf16[512,4,128]{2,1,0:T(4,128)(2,1)S(1)}, bf16[512,4,128]{2,1,0:T(4,128)(2,1)}, u32[]{:S(2)}) %copy-start.9) | copy-done | bytes 524312
  58.3 1.0 %copy-done.10 = f32[2,4,128,128]{3,2,1,0:T(8,128)S(1)} copy-done((f32[2,4,128,128]{3,2,1,0:T(8,128)S(1)}, f32[2,4,128,128]{3,2,1,0:T(8,128)}, u32[]{:S(2)}) %copy-start.10) | copy-done | bytes 524312
  59.3 0.9 copy-done.11
  60.2 0.9 copy-done.12
  61.1 0.7 copy-done.15
  61.8 0.7 copy-done.17
  62.5 4.6 %local.1 = (f32[4,512,128]{2,1,0:T(8,128)S(1)}, bf16[4,512,128]{2,1,0:T(8,128)(2,1)S(1)}, f32[512,8]{1,0:T(8,128)S(1)}, f32[8,8,128]{2,1,0:T(8,128)S(1)}, f32[8,...) custom-call(s32[4]{0:T(128)S(1)} %copy-done.7, s32[4]{0:T(128)S(1)} %copy-done.8, s32[2]{0:T(128)S(1)} %copy-done.21, ...), custom_call_target="tpu_custom_call" | custom-call | flops 2000000000 | bytes 4194304 | tf_op jit(solution)/shard_map/local/pallas_call | solution.py:435
  67.1 6.1 %all-to-all-done.1.got = f32[64,16,128]{2,1,0:T(8,128)S(1)} async-done(((f32[64,16,128]{2,1,0:T(8,128)}), f32[64,16,128]{2,1,0:T(8,128)S(1)}, u32[]{:S(2)}, u32[]{:S(2)}) %all-to-all-start.1) | async-done | bytes 524320 | tf_op jit(solution)/shard_map/all_to_all | solution.py:518
  73.2 0.7 mix.1
  73.9 17.9 %all_to_all.16.got = f32[8,1,640]{2,1,0:T(1,128)S(1)} all-to-all(f32[8,1,640]{2,1,0:T(1,128)S(1)} %get-tuple-element.23), channel_id=1, replica_groups=mesh['ctx'=64,'head'=8] {'head'}, dimensions={0} | all-to-all | bytes 40960 | tf_op jit(solution)/shard_map/all_to_all | solution.py:530
  91.8 1.4 %norm.1 = (bf16[512,4,128]{2,1,0:T(4,128)(2,1)}, bf16[8,2,4,128]{3,2,1,0:T(4,128)(2,1)}) custom-call(f32[8,1,640]{2,1,0:T(1,128)S(1)} %all_to_all.16.got, f32[4,512,128]{2,1,0:T(8,128)S(1)} %get-tuple-element.24.mixed, f32[8,8,128]{2,1,0:T(8,128)S(1)} %get-tuple-element.25.reads), custom_call_target="tpu_custom_call" | custom-call | bytes 4194304 | tf_op jit(solution)/shard_map/norm/pallas_call | solution.py:435
  (29 shorter events, 0.1 us)
Async XLA Ops:
  0.6 0.7 copy-start.7
  1.3 1.0 %copy-start = (bf16[512,4,128]{2,1,0:T(4,128)(2,1)S(1)}, bf16[512,4,128]{2,1,0:T(4,128)(2,1)}, u32[]{:S(2)}) copy-start(bf16[512,4,128]{2,1,0:T(4,128)(2,1)} %key.3) | copy-start | bytes 1572868
  2.3 1.0 %copy-start.2 = (bf16[512,4,128]{2,1,0:T(4,128)(2,1)S(1)}, bf16[512,4,128]{2,1,0:T(4,128)(2,1)}, u32[]{:S(2)}) copy-start(bf16[512,4,128]{2,1,0:T(4,128)(2,1)} %value.3) | copy-start | bytes 1572868
  3.4 0.7 copy-start.4
  4.1 0.7 copy-start.6
  7.8 37.3 %copy-start.16 = (f32[8,512]{1,0:T(8,128)}, f32[8,512]{1,0:T(8,128)S(1)}, u32[]{:S(2)}) copy-start(f32[8,512]{1,0:T(8,128)S(1)} %get-tuple-element.17.running_in) | copy-start | bytes 49156
  7.8 37.3 %copy-start.8 = (s32[4]{0:T(128)S(1)}, s32[4]{0:T(128)}, u32[]{:S(2)}) copy-start(s32[4]{0:T(128)} %owner.3) | copy-start | bytes 52
  45.1 11.5 %copy-start.5 = (bf16[8,2,4,128]{3,2,1,0:T(4,128)(2,1)S(1)}, bf16[8,2,4,128]{3,2,1,0:T(4,128)(2,1)}, u32[]{:S(2)}) copy-start(bf16[8,2,4,128]{3,2,1,0:T(4,128)(2,1)} %step_query.3) | copy-start | bytes 49156
  45.1 11.5 %copy-start.13 = (bf16[8,2,8,128]{3,2,1,0:T(8,128)(2,1)S(1)}, bf16[8,2,8,128]{3,2,1,0:T(8,128)(2,1)}, u32[]{:S(2)}) copy-start(bf16[8,2,8,128]{3,2,1,0:T(8,128)(2,1)} %soft_query.1) | copy-start | bytes 98308
  45.1 11.5 %copy-start.14 = (bf16[8,2,4,128]{3,2,1,0:T(4,128)(2,1)S(1)}, bf16[8,2,4,128]{3,2,1,0:T(4,128)(2,1)}, u32[]{:S(2)}) copy-start(bf16[8,2,4,128]{3,2,1,0:T(4,128)(2,1)} %step_key.1) | copy-start | bytes 49156
  45.1 11.5 %copy-start.20 = (bf16[8,2,1,128]{3,1,2,0:T(2,128)(2,1)S(1)}, bf16[8,2,1,128]{3,1,2,0:T(2,128)(2,1)}, u32[]{:S(2)}) copy-start(bf16[8,2,1,128]{3,1,2,0:T(2,128)(2,1)} %param.32) | copy-start | bytes 12292
  48.3 8.3 %copy-start.1 = (bf16[512,4,128]{2,1,0:T(4,128)(2,1)S(1)}, bf16[512,4,128]{2,1,0:T(4,128)(2,1)}, u32[]{:S(2)}) copy-start(bf16[512,4,128]{2,1,0:T(4,128)(2,1)} %key.3) | copy-start | bytes 1572868
  48.3 8.3 %copy-start.3 = (bf16[512,4,128]{2,1,0:T(4,128)(2,1)S(1)}, bf16[512,4,128]{2,1,0:T(4,128)(2,1)}, u32[]{:S(2)}) copy-start(bf16[512,4,128]{2,1,0:T(4,128)(2,1)} %value.3) | copy-start | bytes 1572868
  48.3 24.9 %all-to-all-start.1 = ((f32[64,16,128]{2,1,0:T(8,128)}), f32[64,16,128]{2,1,0:T(8,128)S(1)}, u32[]{:S(2)}, u32[]{:S(2)}) async-start(f32[64,16,128]{2,1,0:T(8,128)} %scan.1), calls=%async_computation.1 | async-start | bytes 1048576 | tf_op jit(solution)/shard_map/all_to_all | solution.py:518
  56.5 0.7 copy-start.19
  56.5 0.7 copy-start.18
  56.5 0.7 copy-start.21
  57.2 1.0 %copy-start.9 = (bf16[512,4,128]{2,1,0:T(4,128)(2,1)S(1)}, bf16[512,4,128]{2,1,0:T(4,128)(2,1)}, u32[]{:S(2)}) copy-start(bf16[512,4,128]{2,1,0:T(4,128)(2,1)} %query.1) | copy-start | bytes 1572868
  58.3 1.0 %copy-start.10 = (f32[2,4,128,128]{3,2,1,0:T(8,128)S(1)}, f32[2,4,128,128]{3,2,1,0:T(8,128)}, u32[]{:S(2)}) copy-start(f32[2,4,128,128]{3,2,1,0:T(8,128)} %decode_state.1) | copy-start | bytes 1572868
  59.3 0.9 copy-start.11
  60.2 0.9 copy-start.12
  61.1 0.7 copy-start.15
  61.8 0.7 copy-start.17

commit v2 on v1

--- a/solution.py
+++ b/solution.py
@@ -14,9 +14,9 @@
 HD = 128
 HALF = HD // 2
 ROW_END = 8
-ROW_QUERY = 24
-ROW_DECAY = 26
-ROWS_OUT = 32
+ROW_QUERY = 16
+ROW_DECAY = 18
+ROWS_OUT = 19
 ROWS_BACK = 16
 NT = (((1,), (1,)), ((), ()))
 TN = (((0,), (0,)), ((), ()))
@@ -86,6 +86,22 @@
     split = chunks.reshape(8, 2, 8, HD)
     low, high = swap_halves(split[:, 0], split[:, 1])
     return jnp.stack([low, high], axis=1).reshape(HD, HD)
+
+
+def running_sums(decay):
+    heads, block = decay.shape
+    upto = (iota((HD, 1), 0) <= iota((1, HD), 1)).astype(f32).astype(bf16)
+    pieces = [decay[:, low : low + HD] for low in range(0, block, HD)]
+    stacked = jnp.concatenate(pieces, axis=0)
+    local = sum(mm(part, upto) for part in three(stacked))
+    out, before = [], None
+    for k in range(len(pieces)):
+        piece = local[k * heads : (k + 1) * heads]
+        if before is not None:
+            piece = piece + before
+        out.append(piece)
+        before = piece[:, HD - 1 : HD]
+    return jnp.concatenate(out, axis=1)
 
 
 def end_slot(slot, ends, block_start, block):
@@ -100,119 +116,166 @@
     return prompt, offset
 
 
-def summary_kernel(lengths, decay, key, value, step_query, out, running_out):
-    heads, block = decay.shape
+def block_shares(first, second, block):
+    inside = (lax.rem(first, block) != 0) & (lax.rem(second, block) != 0)
+    return inside & (first // block == second // block)
+
+
+def summary_kernel(
+    lengths,
+    decay,
+    key,
+    value,
+    step_query,
+    out,
+    second_out,
+    shared_out,
+    key_buf,
+    value_buf,
+    decay_buf,
+    query_buf,
+    sems,
+):
+    copies = [
+        pltpu.make_async_copy(decay, decay_buf, sems.at[0]),
+        pltpu.make_async_copy(step_query, query_buf, sems.at[1]),
+    ]
+    heads, block = decay_buf.shape
+    quarter = block // 4
+    for k in range(4):
+        part = pl.ds(k * quarter, quarter)
+        copies.append(pltpu.make_async_copy(key.at[part], key_buf.at[part], sems.at[2 + k]))
+        copies.append(pltpu.make_async_copy(value.at[part], value_buf.at[part], sems.at[6 + k]))
+    for copy in copies:
+        copy.start()
+
     block_start = lax.axis_index("ctx") * block
     _, ends = prompt_bounds(lengths)
+    shared = jnp.bool_(False)
+    for other in range(0, len(ends), 2):
+        shared = shared | block_shares(ends[1], ends[other], block)
+    shared_out[0] = shared.astype(jnp.int32)
     place = iota((1, block), 1)
     segment = segment_of(place + block_start, ends)
     last = scalar_segment(block_start + block - 1, ends)
     prompt_a, offset_a = end_slot(0, ends, block_start, block)
     prompt_b, offset_b = end_slot(1, ends, block_start, block)
-
-    parts = jnp.concatenate(three(decay[...]), axis=0)
-    upto = (iota((block, block), 0) <= iota((block, block), 1)).astype(f32).astype(bf16)
-    sums = mm(parts, upto)
-    running = sums[:heads] + sums[heads : 2 * heads] + sums[2 * heads :]
-    running_out[...] = jnp.concatenate([running, running], axis=0)
-
-    row = iota((8, block), 0)
-    spot = iota((8, block), 1)
-    span = jnp.where(
-        row == 0,
-        (jnp.broadcast_to(segment, (8, block)) == last).astype(f32),
-        jnp.where(
-            row == 1,
-            (spot <= offset_a).astype(f32),
-            jnp.where(row == 2, (spot <= offset_b).astype(f32), 0.0),
-        ),
-    )
-    spans = mm(span.astype(bf16), parts, NT)
-    totals = spans[:, :heads] + spans[:, heads : 2 * heads] + spans[:, 2 * heads :]
-    totals = jnp.concatenate([totals, jnp.zeros((8, HD - heads), f32)], axis=1)
-    out[:, ROW_QUERY:ROWS_OUT, :] = jnp.zeros((out.shape[0], ROWS_OUT - ROW_QUERY, HD), f32)
-    out[:, ROW_DECAY : ROW_DECAY + 3, :] = jnp.broadcast_to(
-        totals[None, 0:3], (out.shape[0], 3, HD)
-    )
+    both = (prompt_a >= 0) & (prompt_b >= 0)
+    prompt_a = jnp.where(prompt_a >= 0, prompt_a, prompt_b)
+    offset_a = jnp.where(offset_a >= 0, offset_a, offset_b)
+    copies[0].wait()
+    running = running_sums(decay_buf[...])
 
     def weight(prompt, offset):
         inside = segment == prompt
         at = jnp.sum(jnp.where(place == offset, running, 0.0), axis=1, keepdims=True)
-        return jnp.where(inside, jnp.exp(jnp.where(inside, at - running, 0.0)), 0.0)
+        weight = jnp.where(inside, jnp.exp(jnp.where(inside, at - running, 0.0)), 0.0)
+        return weight, at
+
+    weight_last, _ = weight(last, jnp.int32(block - 1))
+    weight_a, at_a = weight(prompt_a, offset_a)
+    weight_b, at_b = weight(prompt_b, offset_b)
+    whole = jnp.sum(jnp.where(segment == last, decay_buf[...], 0.0), axis=1, keepdims=True)
+    lane, head = iota((heads, HD), 1), iota((heads, HD), 0)
+    totals = jnp.where(lane == head, whole, 0.0)
+    totals = jnp.where(lane == heads + head, at_a, totals)
+    totals = jnp.where(lane == 2 * heads + head, at_b, totals)
+    totals = jnp.sum(totals, axis=0, keepdims=True)
+    out[:, ROW_DECAY, 0, :] = jnp.broadcast_to(totals, (out.shape[0], HD))
 
     weights = jnp.concatenate(
         [
-            weight(last, jnp.int32(block - 1)),
-            weight(prompt_a, offset_a),
-            weight(prompt_b, offset_b),
+            weight_last,
+            weight_a,
+            weight_b,
             jnp.zeros((4, block), f32),
         ],
         axis=0,
     )
     columns = weights.T
 
-    keys = jnp.swapaxes(key[...], 0, 1)
-    values = jnp.swapaxes(value[...], 0, 1)
-    for h in range(heads):
-        value_h = values[h].astype(f32)
-        right = []
-        for k in range(3):
-            c = k * heads + h
-            right.extend(two(value_h * columns[:, c : c + 1]))
-        product = mm(keys[h], jnp.concatenate(right, axis=1), TN)
-        for k in range(3):
-            low = 2 * k * HD
-            state = product[:, low : low + HD] + product[:, low + HD : low + 2 * HD]
-            out[16 * h : 16 * h + 16, 8 * k : 8 * k + 8, :] = cut(state)
-
-    steps, rows = step_query.shape[0], step_query.shape[1]
-    flat = step_query[...].astype(f32).reshape(steps * rows * heads, HD).astype(bf16)
-    d_at, lane = iota((HD, 8 * HD), 0), iota((HD, 8 * HD), 1)
-    pick = (d_at == (lane // HD) * 16 + lane % 16).astype(f32).astype(bf16)
-    spread = mm(flat, pick).reshape(steps, rows * heads, 8 * HD)
-    step_at = iota((steps, 1, 8 * HD), 0)
-    lane3 = iota((steps, 1, 8 * HD), 2)
-    spread = jnp.sum(jnp.where((lane3 % HD) // 16 == step_at, spread, 0.0), axis=0)
+    copies[1].wait()
+    steps, rows = query_buf.shape[0], query_buf.shape[1]
+    flat = query_buf[...].astype(f32).reshape(steps * rows * heads, HD).astype(bf16)
+    lane = iota((1, 8 * HD), 1)
+    pick = (iota((HD, 1), 0) == (lane // HD) * 16 + lane % 16).astype(f32).astype(bf16)
+    read = mm(flat, pick)
+    spread = None
+    for step in range(steps):
+        mine = (lane % HD) // 16 == step
+        part = jnp.where(mine, read[step * rows * heads : (step + 1) * rows * heads], 0.0)
+        spread = part if spread is None else spread + part
     for r in range(rows):
         for h in range(heads):
             for d in range(8):
                 piece = spread[r * heads + h : r * heads + h + 1, d * HD : (d + 1) * HD]
                 for e in range(2):
-                    j = 16 * h + 2 * d + e
-                    out[j, ROW_QUERY + r : ROW_QUERY + r + 1, :] = piece
-
-
-def local_kernel(
-    lengths,
-    owner,
-    row_lengths,
-    running_in,
-    query,
-    key,
-    value,
-    decode_state,
-    step_query,
-    step_key,
-    step_value,
-    step_decay,
-    soft_query,
-    cache_keys,
-    cache_values,
-    new_keys,
-    new_values,
-    intra_out,
-    query_out,
-    gate_out,
-    base_out,
-    coef_out,
-    soft_out,
-):
+                    out[16 * h + 2 * d + e, ROW_QUERY + r, :, :] = piece
+
+    for copy in copies[2:]:
+        copy.wait()
+    keys = jnp.swapaxes(key_buf[...], 0, 1)
+    values = jnp.swapaxes(value_buf[...], 0, 1)
+    for h in range(heads):
+        value_h = values[h].astype(f32)
+        right = []
+        for k in range(2):
+            c = k * heads + h
+            right.extend(two(value_h * columns[:, c : c + 1]))
+        product = mm(keys[h], jnp.concatenate(right, axis=1), TN)
+        for k in range(2):
+            low = 2 * k * HD
+            state = product[:, low : low + HD] + product[:, low + HD : low + 2 * HD]
+            out[16 * h : 16 * h + 16, 8 * k : 8 * k + 8, 0, :] = cut(state)
+
+    @pl.when(both)
+    def _():
+        for h in range(heads):
+            c = 2 * heads + h
+            right = jnp.concatenate(two(values[h].astype(f32) * columns[:, c : c + 1]), axis=1)
+            product = mm(keys[h], right, TN)
+            second_out[16 * h : 16 * h + 16] = cut(product[:, :HD] + product[:, HD:])
+
+    @pl.when(jnp.logical_not(both))
+    def _():
+        second_out[...] = jnp.zeros(second_out.shape, f32)
+
+
+def local_kernel(lengths, owner, row_lengths, *refs):
+    count = (len(refs) - 7) // 2
+    sources, outs = refs[:count], refs[count : count + 6]
+    buffers, sems = refs[count + 6 : -1], refs[-1]
+    copies = [
+        pltpu.make_async_copy(source, buffer, sems.at[k])
+        for k, (source, buffer) in enumerate(zip(sources, buffers))
+    ]
+    for copy in copies:
+        copy.start()
+    for copy in copies:
+        copy.wait()
+    (
+        log_decay,
+        query,
+        key,
+        value,
+        decode_state,
+        step_query,
+        step_key,
+        step_value,
+        step_decay,
+        soft_query,
+        cache_keys,
+        cache_values,
+        new_keys,
+        new_values,
+    ) = buffers
+    intra_out, query_out, gate_out, base_out, coef_out, soft_out = outs
     block, heads, _ = query.shape
     device = lax.axis_index("ctx")
     block_start = device * block
     _, ends = prompt_bounds(lengths)
-    running = running_in[...]
-    columns = running.T
+    running = running_sums(log_decay[...])
+    columns = jnp.concatenate([running, running], axis=0).T
     place_row = iota((1, block), 1) + block_start
     place_col = iota((block, 1), 0) + block_start
     segment_row = segment_of(place_row, ends)
@@ -308,78 +371,86 @@
         soft_out[:, r, :, :] = mixed.reshape(steps, group, HD).astype(bf16)
 
 
-def scan_kernel(lengths, owner, got, out, carried):
+def scan_kernel(block, lengths, owner, got, second, out, carried):
     blocks = got.shape[0]
-    block = lengths_block(blocks)
     device = lax.axis_index("ctx")
     head = device // 16
     starts, ends = prompt_bounds(lengths)
     padded = carried.shape[0]
-
-    decays = got[:, ROW_DECAY, :]
+    heads = blocks // 16
+
+    decays = got[:, ROW_DECAY, 0, :]
     decay = jnp.sum(
         jnp.where(iota((blocks, HD), 1) == head, decays, 0.0), axis=1, keepdims=True
     )
     k_at, b_at = iota((blocks, blocks), 0), iota((blocks, blocks), 1)
     later = jnp.concatenate(
         [jnp.where(k_at > b_at, part.astype(f32), 0.0).astype(bf16) for part in three(decay)],
-        axis=1,
-    )
-    earlier = (iota((padded, blocks), 1) < iota((padded, blocks), 0)).astype(f32).astype(bf16)
-    gaps = mm(earlier, later)
-    gap = gaps[:, :blocks] + gaps[:, blocks : 2 * blocks] + gaps[:, 2 * blocks :]
+        axis=0,
+    )
+    earlier = iota((padded, 3 * blocks), 1) % blocks < iota((padded, 3 * blocks), 0)
+    gap = mm(earlier.astype(f32).astype(bf16), later)
     to, frm = iota((padded, blocks), 0), iota((padded, blocks), 1)
     linked = frm < to
     for start in starts:
         restart = start // block
         linked = linked & ~((restart > frm) & (restart < to))
     weight = jnp.where(linked, jnp.exp(jnp.where(linked, gap, 0.0)), 0.0)
-    weights = jnp.concatenate(two(weight), axis=0)
+    high, low = two(weight)
+    weights = jnp.concatenate([high, high, low], axis=1)
+    right = []
     for i in range(8):
-        high, low = two(got[:, i, :])
-        product = mm(weights, jnp.concatenate([high, low], axis=1))
-        state = product[:padded, :HD] + product[padded:, :HD] + product[:padded, HD:]
+        high, low = two(got[:, i, 0, :])
+        right.append(jnp.concatenate([high, low, high], axis=0))
+    product = mm(weights, jnp.concatenate(right, axis=1))
+    for i in range(8):
+        state = product[:, i * HD : (i + 1) * HD]
         carried[:, i, :] = state
-        out[:, i, :] = state[:blocks]
-
-    out[:, 8:ROWS_BACK, :] = jnp.zeros((blocks, ROWS_BACK - 8, HD), f32)
-    rows_n = 2
+        out[:, i, 0, :] = state[:blocks]
+        out[:, 8 + i, 0, :] = jnp.zeros((blocks, HD), f32)
+
+    rows_n = ROW_DECAY - ROW_QUERY
+    steps = 8
+    lane = iota((steps, HD), 1)
+    reads = []
     for p in range(len(ends)):
-        slot = p % 2
         index = ends[p] // block
         source = jnp.minimum(index, blocks - 1)
-        partial = (lax.rem(ends[p], block) != 0).astype(f32)
+        partial = lax.rem(ends[p], block) != 0
         leads = (starts[p] < index * block).astype(f32)
-        run = got[source, ROW_DECAY + 1 + slot : ROW_DECAY + 2 + slot, :]
-        run = jnp.sum(jnp.where(iota((1, HD), 1) == head, run, 0.0), axis=1, keepdims=True)
-        lead = leads * jnp.exp(run * partial)
-        low_row = ROW_END + 8 * slot
-        handed = carried[index] * lead + got[source, low_row : low_row + 8, :] * partial
+        if p % 2:
+            shared = jnp.bool_(False)
+            for other in range(0, len(ends), 2):
+                shared = shared | block_shares(ends[p], ends[other], block)
+        else:
+            shared = jnp.bool_(False)
+        run = got[source, ROW_DECAY, :, :]
+        at = jnp.where(shared, 2 * heads, heads) + head
+        run = jnp.sum(jnp.where(iota((1, HD), 1) == at, run, 0.0), axis=1, keepdims=True)
+        lead = leads * jnp.exp(jnp.where(partial, run, 0.0))
+        rest = got[source, ROW_END : ROW_END + 8, 0, :]
+        if p % 2:
+            rest = jnp.where(shared, second[source], rest)
+        handed = carried[index] * lead + jnp.where(partial, rest, 0.0)
         high, low = two(jnp.concatenate([handed[:, :HALF], handed[:, HALF:]], axis=0))
-        right = jnp.concatenate([jnp.concatenate([high, low], axis=1)] * 8, axis=0)
+        both = jnp.concatenate([jnp.concatenate([high, low], axis=1)] * 8, axis=0)
         place = owner[p] // rows_n
         side = lax.rem(owner[p], rows_n)
-        pair = got[place, ROW_QUERY : ROW_QUERY + rows_n, :]
-        query = jnp.where(side == 0, pair[0:1], pair[1:2])
-        steps = 8
-        lane = iota((steps, HD), 1)
+        query = got[place, ROW_QUERY + side, :, :]
         query = jnp.where(lane // 16 == iota((steps, HD), 0), query, 0.0).astype(bf16)
-        read = mm(query, right)
+        read = mm(query, both)
         read = read[:, :HALF] + read[:, HALF:]
-        both = jnp.concatenate([read, read], axis=1)
-        old = out[place, 8:ROWS_BACK, :]
-        out[place, 8:ROWS_BACK, :] = jnp.where(lane // HALF == side, both, old)
-
-
-def lengths_block(blocks):
-    return 512
+        reads.append((place, side, jnp.concatenate([read, read], axis=1)))
+    for place, side, read in reads:
+        old = out[place, 8:ROWS_BACK, 0, :]
+        out[place, 8:ROWS_BACK, 0, :] = jnp.where(lane // HALF == side, read, old)
 
 
 def mix_kernel(got, intra, query, gate, base, coef, mixed_out, reads_out, squares_out):
     heads, block, _ = intra.shape
     total = None
     for h in range(heads):
-        state = uncut(got[16 * h : 16 * h + 16, 0:8, :])
+        state = uncut(got[16 * h : 16 * h + 16, 0:8, 0, :])
         high, low = two(state)
         read = mm(query[h], jnp.concatenate([high, low], axis=1))
         mixed = intra[h] + (read[:, :HD] + read[:, HD:]) * gate[:, h : h + 1]
@@ -394,8 +465,8 @@
     for h in range(heads):
         first, second = None, None
         for d in range(8):
-            a = got[16 * h + 2 * d, 8:16, :]
-            b = got[16 * h + 2 * d + 1, 8:16, :]
+            a = got[16 * h + 2 * d, 8:16, 0, :]
+            b = got[16 * h + 2 * d + 1, 8:16, 0, :]
             first = a if first is None else first + a
             second = b if second is None else second + b
         for r, handed in enumerate(swap_halves(first, second)):
@@ -428,16 +499,22 @@
     decode_out[...] = scaled.reshape(decode_out.shape).astype(bf16)
 
 
-def call(kernel, name, outs, scalars, arrays, scratch=(), cost=0):
+def call(kernel, name, outs, scalars, arrays, scratch=(), cost=0, space=pltpu.VMEM):
+    scalars = [pltpu.with_memory_space_constraint(x, pltpu.HBM) for x in scalars]
+    if space is pltpu.HBM:
+        arrays = [pltpu.with_memory_space_constraint(x, space) for x in arrays]
     shapes = [jax.ShapeDtypeStruct(shape, dtype) for shape, dtype in outs]
     specs = [pl.BlockSpec(memory_space=pltpu.SMEM)] * len(scalars)
-    specs += [pl.BlockSpec(memory_space=pltpu.VMEM)] * len(arrays)
+    specs += [pl.BlockSpec(memory_space=space)] * len(arrays)
     return pl.pallas_call(
         kernel,
         name=name,
         out_shape=shapes,
         in_specs=specs,
-        out_specs=[pl.BlockSpec(memory_space=pltpu.VMEM)] * len(outs),
+        out_specs=[
+            pl.BlockSpec(memory_space=pltpu.SMEM if dtype == jnp.int32 else pltpu.VMEM)
+            for _, dtype in outs
+        ],
         scratch_shapes=list(scratch),
         compiler_params=pltpu.CompilerParams(vmem_limit_bytes=24 * 2**20),
         cost_estimate=pl.CostEstimate(flops=cost, bytes_accessed=4 * 2**20, transcendentals=0),
@@ -469,14 +546,48 @@
     planes = lax.axis_size("head")
     pairs = rows_n * heads
     decay_rows = jnp.swapaxes(log_decay, 0, 1)
-    outgoing, running = call(
+    outgoing, second, shared = call(
         summary_kernel,
         "summary",
-        [((blocks, ROWS_OUT, HD), f32), ((8, block), f32)],
+        [
+            ((blocks, ROWS_OUT, 1, HD), f32),
+            ((blocks, 8, HD), f32),
+            ((1,), jnp.int32),
+        ],
         [lengths],
         [decay_rows, prefill_key, prefill_value, step_query],
+        scratch=[
+            pltpu.VMEM(prefill_key.shape, bf16),
+            pltpu.VMEM(prefill_value.shape, bf16),
+            pltpu.VMEM(decay_rows.shape, f32),
+            pltpu.VMEM(step_query.shape, bf16),
+            pltpu.SemaphoreType.DMA((10,)),
+        ],
+        space=pltpu.HBM,
     )
     gathered = lax.all_to_all(outgoing, "ctx", 0, 0, tiled=True)
+    second = lax.cond(
+        shared[0] > 0,
+        lambda x: lax.all_to_all(x, "ctx", 0, 0, tiled=True),
+        lambda x: x,
+        second,
+    )
+    local_inputs = [
+        decay_rows,
+        prefill_query,
+        prefill_key,
+        prefill_value,
+        decode_state,
+        step_query,
+        step_key,
+        step_value,
+        jnp.transpose(step_decay, (1, 2, 0)),
+        soft_query,
+        cache_keys.reshape(rows_n, -1, HD),
+        cache_values.reshape(rows_n, -1, HD),
+        new_keys.reshape(steps, rows_n, HD),
+        new_values.reshape(steps, rows_n, HD),
+    ]
     intra, queries, gate, base, coef, soft_out = call(
         local_kernel,
         "local",
@@ -489,30 +600,18 @@
             (soft_query.shape, bf16),
         ],
         [lengths, owner, row_lengths],
-        [
-            running,
-            prefill_query,
-            prefill_key,
-            prefill_value,
-            decode_state,
-            step_query,
-            step_key,
-            step_value,
-            jnp.transpose(step_decay, (1, 2, 0)),
-            soft_query,
-            cache_keys.reshape(rows_n, -1, HD),
-            cache_values.reshape(rows_n, -1, HD),
-            new_keys.reshape(steps, rows_n, HD),
-            new_values.reshape(steps, rows_n, HD),
-        ],
+        local_inputs,
+        scratch=[pltpu.VMEM(x.shape, x.dtype) for x in local_inputs]
+        + [pltpu.SemaphoreType.DMA((len(local_inputs),))],
         cost=2 * 10**9,
+        space=pltpu.HBM,
     )
     returning = call(
-        scan_kernel,
+        functools.partial(scan_kernel, block),
         "scan",
-        [((blocks, ROWS_BACK, HD), f32)],
+        [((blocks, ROWS_BACK, 1, HD), f32)],
         [lengths, owner],
-        [gathered],
+        [gathered, second],
         scratch=[pltpu.VMEM((blocks + 8, 8, HD), f32)],
     )[0]
     returned = lax.all_to_all(returning, "ctx", 0, 0, tiled=True)

time: 94.1 us -> 83.3 us (0.89)
  local copies, waits for them, and re-layouts: 10.1 us -> 0 us
  blocking collectives: 55.2 us -> 47.1 us
  Pallas kernels: 12.8 us -> 17.5 us
  waiting for transfers between devices: 6.09 us -> 9.7 us
  starting transfers between devices: 8.23 us -> 7.06 us
    unnamed x44 -> x0, local copies, waits for them, and re-layouts: 10.1 us -> none
    all_to_all x1, blocking collectives: 37.3 us -> 29.2 us  [body(): gathered = lax.all_to_all(outgoing, 'ctx', 0, 0, tiled=True)]
    pallas_call x5, Pallas kernels: 12.8 us -> 17.5 us  [call(): pl.pallas_call(kernel, name=name, out_shape=shapes, in_specs=specs, out_s...]
    all_to_all x1, waiting for transfers between devices: 6.09 us -> 9.7 us  [body(): returned = lax.all_to_all(returning, 'ctx', 0, 0, tiled=True)]
    all_to_all x1, starting transfers between devices: 8.23 us -> 7.06 us  [body(): returned = lax.all_to_all(returning, 'ctx', 0, 0, tiled=True)]
  transfers between devices with their start and end apart: 1 -> 1, of which waited for: 1 -> 1; matrix products, arithmetic and copies ran while one was open for 0% -> 0% of each run, Pallas kernels for 5% -> 8%
where the time goes in v2:
time: 83.3 us; the launch traced here: 82.7 us
  blocking collectives  47.1 us (57%)
  Pallas kernels  17.5 us (21%)
  waiting for transfers between devices  9.7 us (12%)
  starting transfers between devices  7.06 us (8%)
  between operations  1.31 us (2%)
    all_to_all x1, blocking collectives, body(): gathered = lax.all_to_all(outgoing, 'ctx', 0, 0, tiled=True)  29.2 us
    all_to_all x1, blocking collectives, body(): squares = lax.all_to_all(squares, 'head', 0, 0, tiled=True)  17.9 us
    pallas_call x5, Pallas kernels, call(): pl.pallas_call(kernel, name=name, out_shape=shapes, in_specs=specs, out_s...  17.5 us
    all_to_all x1, waiting for transfers between devices, body(): returned = lax.all_to_all(returning, 'ctx', 0, 0, tiled=True)  9.7 us
    all_to_all x1, starting transfers between devices, body(): returned = lax.all_to_all(returning, 'ctx', 0, 0, tiled=True)  7.06 us
  transfers between devices with their start and end apart: 1, of which 1 were waited for; matrix products, arithmetic and copies ran while one was open for 0% of the time, Pallas kernels for 8%

profile of v2, /device:TPU:6, one launch (start us, length us, event | category | flops | bytes accessed | tf_op | source)
XLA Modules:
  0.0 82.7 jit_solution(16425069191160147229)
XLA Ops:
  0.6 5.1 %summary.1 = (f32[64,19,1,128]{3,2,1,0:T(1,128)S(1)}, f32[64,8,128]{2,1,0:T(8,128)S(1)}, s32[1]{0:T(128)}) custom-call(s32[4]{0:T(128)} %lengths.5, f32[4,512]{1,0:T(4,128)} %bitcast.7, bf16[512,4,128]{2,1,0:T(4,128)(2,1)} %refs_2_.1, bf16[512,4,128]{2,1,0:T(4,128)(2,1)} %refs_3_.1, bf16[8,2,4,128]{3,2,1,0:T(4,128)(2,1)} %refs_5_.1), custom_call_target="tpu_custom_call" | custom-call | bytes 4194304 | tf_op jit(solution)/shard_map/summary/pallas_call | solution.py:509
  6.4 29.2 %all_to_all.20.got = f32[64,19,1,128]{3,2,1,0:T(1,128)S(1)} all-to-all(f32[64,19,1,128]{3,2,1,0:T(1,128)S(1)} %get-tuple-element.22), channel_id=1, replica_groups=mesh['ctx'=64,'head'=8] {'ctx'}, dimensions={0} | all-to-all | bytes 1245184 | tf_op jit(solution)/shard_map/all_to_all | solution.py:568
  35.7 3.2 %scan.1 = f32[64,16,1,128]{3,2,1,0:T(1,128)} custom-call(s32[4]{0:T(128)} %lengths.5, s32[4]{0:T(128)} %owner.3, f32[64,19,1,128]{3,2,1,0:T(1,128)S(1)} %all_to_all.20.got, f32[64,8,128]{2,1,0:T(8,128)S(1)} %get-tuple-element.36.second), custom_call_target="tpu_custom_call" | custom-call | bytes 4194304 | tf_op jit(solution)/shard_map/scan/pallas_call | solution.py:509
  38.9 7.1 %all-to-all-start.2 = ((f32[64,16,1,128]{3,2,1,0:T(1,128)}), f32[64,16,1,128]{3,2,1,0:T(1,128)S(1)}, u32[]{:S(2)}, u32[]{:S(2)}) async-start(f32[64,16,1,128]{3,2,1,0:T(1,128)} %scan.1), calls=%async_computation.2 | async-start | bytes 1048576 | tf_op jit(solution)/shard_map/all_to_all | solution.py:617
  45.9 7.0 %local.1 = (f32[4,512,128]{2,1,0:T(8,128)S(1)}, bf16[4,512,128]{2,1,0:T(8,128)(2,1)S(1)}, f32[512,8]{1,0:T(8,128)S(1)}, f32[8,8,128]{2,1,0:T(8,128)S(1)}, f32[8,...) custom-call(s32[4]{0:T(128)} %lengths.5, s32[4]{0:T(128)} %owner.3, s32[2]{0:T(128)} %row_lengths.1, f32[4,512]{1,0:T(4,128)} %bitcast.8, ...), custom_call_target="tpu_custom_call" | custom-call | flops 2000000000 | bytes 4194304 | tf_op jit(solution)/shard_map/local/pallas_call | solution.py:509
  53.0 9.7 %all-to-all-done.2.got = f32[64,16,1,128]{3,2,1,0:T(1,128)S(1)} async-done(((f32[64,16,1,128]{3,2,1,0:T(1,128)}), f32[64,16,1,128]{3,2,1,0:T(1,128)S(1)}, u32[]{:S(2)}, u32[]{:S(2)}) %all-to-all-start.2) | async-done | bytes 524320 | tf_op jit(solution)/shard_map/all_to_all | solution.py:617
  62.7 0.8 mix.1
  63.5 17.9 %all_to_all.21.got = f32[8,1,640]{2,1,0:T(1,128)S(1)} all-to-all(f32[8,1,640]{2,1,0:T(1,128)S(1)} %get-tuple-element.30), channel_id=1, replica_groups=mesh['ctx'=64,'head'=8] {'head'}, dimensions={0} | all-to-all | bytes 40960 | tf_op jit(solution)/shard_map/all_to_all | solution.py:629
  81.4 1.4 %norm.1 = (bf16[512,4,128]{2,1,0:T(4,128)(2,1)}, bf16[8,2,4,128]{3,2,1,0:T(4,128)(2,1)}) custom-call(f32[8,1,640]{2,1,0:T(1,128)S(1)} %all_to_all.21.got, f32[4,512,128]{2,1,0:T(8,128)S(1)} %get-tuple-element.31.mixed, f32[8,8,128]{2,1,0:T(8,128)S(1)} %get-tuple-element.32.reads), custom_call_target="tpu_custom_call" | custom-call | bytes 4194304 | tf_op jit(solution)/shard_map/norm/pallas_call | solution.py:509
  (1 shorter events, 0.0 us)
Async XLA Ops:
  38.9 23.8 %all-to-all-start.2 = ((f32[64,16,1,128]{3,2,1,0:T(1,128)}), f32[64,16,1,128]{3,2,1,0:T(1,128)S(1)}, u32[]{:S(2)}, u32[]{:S(2)}) async-start(f32[64,16,1,128]{3,2,1,0:T(1,128)} %scan.1), calls=%async_computation.2 | async-start | bytes 1048576 | tf_op jit(solution)/shard_map/all_to_all | solution.py:617

commit v3 on v2

--- a/solution.py
+++ b/solution.py
@@ -12,12 +12,12 @@
 bf16 = jnp.bfloat16
 eps = 1e-06
 HD = 128
-HALF = HD // 2
+QUARTER = HD // 4
 ROW_END = 8
 ROW_QUERY = 16
-ROW_DECAY = 18
-ROWS_OUT = 19
-ROWS_BACK = 16
+ROW_DECAY = 20
+ROWS_OUT = 21
+ROWS_BACK = 12
 NT = (((1,), (1,)), ((), ()))
 TN = (((0,), (0,)), ((), ()))
 NN = (((1,), (0,)), ((), ()))
@@ -67,25 +67,29 @@
     return segment
 
 
-def swap_halves(first, second):
-    left = iota((1, HD), 1) < HALF
+def swap(first, second, width):
     shape = first.shape
-    rolled_first = pltpu.roll(first.reshape(-1, HD), HALF, 1).reshape(shape)
-    rolled_second = pltpu.roll(second.reshape(-1, HD), HALF, 1).reshape(shape)
-    left = left.reshape((1,) * (len(shape) - 1) + (HD,))
-    return jnp.where(left, first, rolled_second), jnp.where(left, rolled_first, second)
+    even = ((iota((1, HD), 1) // width) % 2 == 0).reshape((1,) * (len(shape) - 1) + (HD,))
+    up = pltpu.roll(second.reshape(-1, HD), width, 1).reshape(shape)
+    down = pltpu.roll(first.reshape(-1, HD), HD - width, 1).reshape(shape)
+    return jnp.where(even, first, up), jnp.where(even, down, second)
+
+
+def turn(a, b, c, d):
+    a, c = swap(a, c, 2 * QUARTER)
+    b, d = swap(b, d, 2 * QUARTER)
+    a, b = swap(a, b, QUARTER)
+    c, d = swap(c, d, QUARTER)
+    return a, b, c, d
 
 
 def cut(matrix):
-    split = matrix.reshape(8, 2, 8, HD)
-    low, high = swap_halves(split[:, 0], split[:, 1])
-    return jnp.stack([low, high], axis=1).reshape(16, 8, HD)
+    split = matrix.reshape(4, 4, 8, HD)
+    return jnp.stack(turn(*(split[:, k] for k in range(4))), axis=1).reshape(16, 8, HD)
 
 
 def uncut(chunks):
-    split = chunks.reshape(8, 2, 8, HD)
-    low, high = swap_halves(split[:, 0], split[:, 1])
-    return jnp.stack([low, high], axis=1).reshape(HD, HD)
+    return cut(chunks.reshape(HD, HD)).reshape(HD, HD)
 
 
 def running_sums(decay):
@@ -122,7 +126,7 @@
 
 
 def summary_kernel(
-    lengths,
+    lengths_in,
     decay,
     key,
     value,
@@ -134,6 +138,7 @@
     value_buf,
     decay_buf,
     query_buf,
+    lengths,
     sems,
 ):
     copies = [
@@ -146,10 +151,12 @@
         part = pl.ds(k * quarter, quarter)
         copies.append(pltpu.make_async_copy(key.at[part], key_buf.at[part], sems.at[2 + k]))
         copies.append(pltpu.make_async_copy(value.at[part], value_buf.at[part], sems.at[6 + k]))
+    bounds = pltpu.make_async_copy(lengths_in, lengths, sems.at[10])
+    bounds.start()
     for copy in copies:
         copy.start()
-
     block_start = lax.axis_index("ctx") * block
+    bounds.wait()
     _, ends = prompt_bounds(lengths)
     shared = jnp.bool_(False)
     for other in range(0, len(ends), 2):
@@ -183,58 +190,53 @@
     totals = jnp.sum(totals, axis=0, keepdims=True)
     out[:, ROW_DECAY, 0, :] = jnp.broadcast_to(totals, (out.shape[0], HD))
 
-    weights = jnp.concatenate(
-        [
-            weight_last,
-            weight_a,
-            weight_b,
-            jnp.zeros((4, block), f32),
-        ],
-        axis=0,
-    )
-    columns = weights.T
-
     copies[1].wait()
     steps, rows = query_buf.shape[0], query_buf.shape[1]
-    flat = query_buf[...].astype(f32).reshape(steps * rows * heads, HD).astype(bf16)
-    lane = iota((1, 8 * HD), 1)
-    pick = (iota((HD, 1), 0) == (lane // HD) * 16 + lane % 16).astype(f32).astype(bf16)
-    read = mm(flat, pick)
-    spread = None
-    for step in range(steps):
-        mine = (lane % HD) // 16 == step
-        part = jnp.where(mine, read[step * rows * heads : (step + 1) * rows * heads], 0.0)
-        spread = part if spread is None else spread + part
-    for r in range(rows):
-        for h in range(heads):
-            for d in range(8):
-                piece = spread[r * heads + h : r * heads + h + 1, d * HD : (d + 1) * HD]
-                for e in range(2):
-                    out[16 * h + 2 * d + e, ROW_QUERY + r, :, :] = piece
+    pairs = rows * heads
+    flat = query_buf[...].astype(f32).reshape(steps * pairs, HD).astype(bf16)
+    lane = iota((1, 4 * HD), 1)
+    pick = iota((HD, 1), 0) == (lane // HD) * QUARTER + lane % QUARTER
+    read = mm(flat, pick.astype(f32).astype(bf16))
+    spread = []
+    for k in range(2):
+        total = None
+        for step in range(4):
+            low = (4 * k + step) * pairs
+            mine = (lane % HD) // QUARTER == step
+            part = jnp.where(mine, read[low : low + pairs], 0.0)
+            total = part if total is None else total + part
+        spread.append(total)
+    spread = jnp.concatenate(spread, axis=0).reshape(2 * rows, heads, 4 * HD)
+    spread = jnp.swapaxes(spread, 0, 1)
+    for h in range(heads):
+        for d in range(4):
+            piece = spread[h, :, d * HD : (d + 1) * HD]
+            j = 16 * h + 4 * d
+            out[j : j + 4, ROW_QUERY:ROW_DECAY, 0, :] = jnp.broadcast_to(
+                piece[None], (4, 2 * rows, HD)
+            )
 
     for copy in copies[2:]:
         copy.wait()
     keys = jnp.swapaxes(key_buf[...], 0, 1)
     values = jnp.swapaxes(value_buf[...], 0, 1)
     for h in range(heads):
-        value_h = values[h].astype(f32)
-        right = []
-        for k in range(2):
-            c = k * heads + h
-            right.extend(two(value_h * columns[:, c : c + 1]))
-        product = mm(keys[h], jnp.concatenate(right, axis=1), TN)
+        key_h = keys[h].T.astype(f32)
+        left = []
+        for weight_k in (weight_last, weight_a):
+            left.extend(two(key_h * weight_k[h : h + 1]))
+        product = mm(jnp.concatenate(left, axis=0), values[h])
         for k in range(2):
             low = 2 * k * HD
-            state = product[:, low : low + HD] + product[:, low + HD : low + 2 * HD]
+            state = product[low : low + HD] + product[low + HD : low + 2 * HD]
             out[16 * h : 16 * h + 16, 8 * k : 8 * k + 8, 0, :] = cut(state)
 
     @pl.when(both)
     def _():
         for h in range(heads):
-            c = 2 * heads + h
-            right = jnp.concatenate(two(values[h].astype(f32) * columns[:, c : c + 1]), axis=1)
-            product = mm(keys[h], right, TN)
-            second_out[16 * h : 16 * h + 16] = cut(product[:, :HD] + product[:, HD:])
+            left = two(keys[h].T.astype(f32) * weight_b[h : h + 1])
+            product = mm(jnp.concatenate(left, axis=0), values[h])
+            second_out[16 * h : 16 * h + 16] = cut(product[:HD] + product[HD:])
 
     @pl.when(jnp.logical_not(both))
     def _():
@@ -371,11 +373,18 @@
         soft_out[:, r, :, :] = mixed.reshape(steps, group, HD).astype(bf16)
 
 
-def scan_kernel(block, lengths, owner, got, second, out, carried):
+def scan_kernel(
+    block, lengths_in, owner_in, got, second, out, carried, lengths, owner, sems
+):
+    copies = [
+        pltpu.make_async_copy(lengths_in, lengths, sems.at[0]),
+        pltpu.make_async_copy(owner_in, owner, sems.at[1]),
+    ]
+    for copy in copies:
+        copy.start()
     blocks = got.shape[0]
     device = lax.axis_index("ctx")
     head = device // 16
-    starts, ends = prompt_bounds(lengths)
     padded = carried.shape[0]
     heads = blocks // 16
 
@@ -390,6 +399,15 @@
     )
     earlier = iota((padded, 3 * blocks), 1) % blocks < iota((padded, 3 * blocks), 0)
     gap = mm(earlier.astype(f32).astype(bf16), later)
+    right = []
+    for i in range(8):
+        high, low = two(got[:, i, 0, :])
+        right.append(jnp.concatenate([high, low, high], axis=0))
+    right = jnp.concatenate(right, axis=1)
+
+    for copy in copies:
+        copy.wait()
+    starts, ends = prompt_bounds(lengths)
     to, frm = iota((padded, blocks), 0), iota((padded, blocks), 1)
     linked = frm < to
     for start in starts:
@@ -398,20 +416,18 @@
     weight = jnp.where(linked, jnp.exp(jnp.where(linked, gap, 0.0)), 0.0)
     high, low = two(weight)
     weights = jnp.concatenate([high, high, low], axis=1)
-    right = []
-    for i in range(8):
-        high, low = two(got[:, i, 0, :])
-        right.append(jnp.concatenate([high, low, high], axis=0))
-    product = mm(weights, jnp.concatenate(right, axis=1))
+    product = mm(weights, right)
     for i in range(8):
         state = product[:, i * HD : (i + 1) * HD]
         carried[:, i, :] = state
         out[:, i, 0, :] = state[:blocks]
-        out[:, 8 + i, 0, :] = jnp.zeros((blocks, HD), f32)
-
-    rows_n = ROW_DECAY - ROW_QUERY
+        if i < ROWS_BACK - 8:
+            out[:, 8 + i, 0, :] = jnp.zeros((blocks, HD), f32)
+
+    rows_n = (ROW_DECAY - ROW_QUERY) // 2
     steps = 8
-    lane = iota((steps, HD), 1)
+    lane, step_at = iota((steps, HD), 1), iota((steps, HD), 0)
+    mine = lane // QUARTER == step_at % 4
     reads = []
     for p in range(len(ends)):
         index = ends[p] // block
@@ -432,18 +448,23 @@
         if p % 2:
             rest = jnp.where(shared, second[source], rest)
         handed = carried[index] * lead + jnp.where(partial, rest, 0.0)
-        high, low = two(jnp.concatenate([handed[:, :HALF], handed[:, HALF:]], axis=0))
-        both = jnp.concatenate([jnp.concatenate([high, low], axis=1)] * 8, axis=0)
+        handed = [handed[:, g * QUARTER : (g + 1) * QUARTER] for g in range(4)]
+        high, low = two(jnp.concatenate(handed, axis=0))
+        both = jnp.concatenate([jnp.concatenate([high, low], axis=1)] * 4, axis=0)
         place = owner[p] // rows_n
         side = lax.rem(owner[p], rows_n)
-        query = got[place, ROW_QUERY + side, :, :]
-        query = jnp.where(lane // 16 == iota((steps, HD), 0), query, 0.0).astype(bf16)
-        read = mm(query, both)
-        read = read[:, :HALF] + read[:, HALF:]
-        reads.append((place, side, jnp.concatenate([read, read], axis=1)))
+        query = jnp.where(
+            step_at < 4,
+            got[place, ROW_QUERY + side, :, :],
+            got[place, ROW_QUERY + rows_n + side, :, :],
+        )
+        read = mm(jnp.where(mine, query, 0.0).astype(bf16), both)
+        read = read[:, :QUARTER] + read[:, QUARTER:]
+        reads.append((place, side, jnp.concatenate([read[:4], read[4:]] * 2, axis=1)))
     for place, side, read in reads:
         old = out[place, 8:ROWS_BACK, 0, :]
-        out[place, 8:ROWS_BACK, 0, :] = jnp.where(lane // HALF == side, read, old)
+        kept = lane[:4] // (2 * QUARTER) == side
+        out[place, 8:ROWS_BACK, 0, :] = jnp.where(kept, read, old)
 
 
 def mix_kernel(got, intra, query, gate, base, coef, mixed_out, reads_out, squares_out):
@@ -458,27 +479,29 @@
         total = mixed * mixed if total is None else total + mixed * mixed
     ones = jnp.ones((8, HD), bf16)
     high, low = two(total)
-    squares_out[:, 0, :block] = mm(ones, high, NT) + mm(ones, low, NT)
+    planes = squares_out.shape[0]
+    squares_out[:, 0, :block] = (mm(ones, high, NT) + mm(ones, low, NT))[:planes]
 
     rows_n = base.shape[0] // heads
     squares = [None] * rows_n
     for h in range(heads):
-        first, second = None, None
-        for d in range(8):
-            a = got[16 * h + 2 * d, 8:16, 0, :]
-            b = got[16 * h + 2 * d + 1, 8:16, 0, :]
-            first = a if first is None else first + a
-            second = b if second is None else second + b
-        for r, handed in enumerate(swap_halves(first, second)):
+        pieces = []
+        for e in range(4):
+            total = got[16 * h + e, 8:ROWS_BACK, 0, :]
+            for d in range(1, 4):
+                total = total + got[16 * h + 4 * d + e, 8:ROWS_BACK, 0, :]
+            pieces.append(total)
+        pieces = turn(*pieces)
+        for r in range(rows_n):
+            handed = jnp.concatenate(pieces[2 * r : 2 * r + 2], axis=0)
             n = r * heads + h
             read = base[n] + coef[n] * handed
             reads_out[n] = read
             squares[r] = read * read if squares[r] is None else squares[r] + read * read
     high, low = two(jnp.concatenate(squares, axis=0))
     sums = mm(ones, high, NT) + mm(ones, low, NT)
-    squares_out[:, 0, block:] = jnp.concatenate(
-        [sums, jnp.zeros((8, HD - sums.shape[1]), f32)], axis=1
-    )
+    sums = jnp.concatenate([sums, jnp.zeros((8, HD - sums.shape[1]), f32)], axis=1)
+    squares_out[:, 0, block:] = sums[:planes]
 
 
 def norm_kernel(count, got, mixed, reads, prefill_out, decode_out):
@@ -499,12 +522,22 @@
     decode_out[...] = scaled.reshape(decode_out.shape).astype(bf16)
 
 
-def call(kernel, name, outs, scalars, arrays, scratch=(), cost=0, space=pltpu.VMEM):
+def call(
+    kernel,
+    name,
+    outs,
+    scalars,
+    arrays,
+    scratch=(),
+    cost=0,
+    space=pltpu.VMEM,
+    scalar_space=pltpu.HBM,
+):
     scalars = [pltpu.with_memory_space_constraint(x, pltpu.HBM) for x in scalars]
     if space is pltpu.HBM:
         arrays = [pltpu.with_memory_space_constraint(x, space) for x in arrays]
     shapes = [jax.ShapeDtypeStruct(shape, dtype) for shape, dtype in outs]
-    specs = [pl.BlockSpec(memory_space=pltpu.SMEM)] * len(scalars)
+    specs = [pl.BlockSpec(memory_space=scalar_space)] * len(scalars)
     specs += [pl.BlockSpec(memory_space=space)] * len(arrays)
     return pl.pallas_call(
         kernel,
@@ -561,7 +594,8 @@
             pltpu.VMEM(prefill_value.shape, bf16),
             pltpu.VMEM(decay_rows.shape, f32),
             pltpu.VMEM(step_query.shape, bf16),
-            pltpu.SemaphoreType.DMA((10,)),
+            pltpu.SMEM(lengths.shape, jnp.int32),
+            pltpu.SemaphoreType.DMA((11,)),
         ],
         space=pltpu.HBM,
     )
@@ -605,14 +639,21 @@
         + [pltpu.SemaphoreType.DMA((len(local_inputs),))],
         cost=2 * 10**9,
         space=pltpu.HBM,
-    )
+        scalar_space=pltpu.SMEM,
+    )
+    gathered, intra = lax.optimization_barrier((gathered, intra))
     returning = call(
         functools.partial(scan_kernel, block),
         "scan",
         [((blocks, ROWS_BACK, 1, HD), f32)],
         [lengths, owner],
         [gathered, second],
-        scratch=[pltpu.VMEM((blocks + 8, 8, HD), f32)],
+        scratch=[
+            pltpu.VMEM((blocks + 8, 8, HD), f32),
+            pltpu.SMEM(lengths.shape, jnp.int32),
+            pltpu.SMEM(owner.shape, jnp.int32),
+            pltpu.SemaphoreType.DMA((2,)),
+        ],
     )[0]
     returned = lax.all_to_all(returning, "ctx", 0, 0, tiled=True)
     mixed, reads, squares = call(

time: 83.3 us -> 79.6 us (0.956)
  blocking collectives: 47.1 us -> 39 us
  starting transfers between devices: 7.06 us -> 10.8 us
  waiting for transfers between devices: 9.7 us -> 12.9 us
  Pallas kernels: 17.5 us -> 15.1 us
    all_to_all x1, blocking collectives: 29.2 us -> 21.1 us  [body(): returned = lax.all_to_all(returning, 'ctx', 0, 0, tiled=True)]
    all_to_all x1, starting transfers between devices: 7.06 us -> 10.8 us  [body(): gathered = lax.all_to_all(outgoing, 'ctx', 0, 0, tiled=True)]
    all_to_all x1, waiting for transfers between devices: 9.7 us -> 12.9 us  [body(): gathered = lax.all_to_all(outgoing, 'ctx', 0, 0, tiled=True)]
    pallas_call x5, Pallas kernels: 17.5 us -> 15.1 us  [call(): pl.pallas_call(kernel, name=name, out_shape=shapes, in_specs=specs, out_s...]
  transfers between devices with their start and end apart: 1 -> 1, of which waited for: 1 -> 1; matrix products, arithmetic and copies ran while one was open for 0% -> 0% of each run, Pallas kernels for 8% -> 9%
where the time goes in v3:
time: 79.6 us; the launch traced here: 79.2 us
  blocking collectives  39 us (49%)
  Pallas kernels  15.1 us (19%)
  waiting for transfers between devices  12.9 us (16%)
  starting transfers between devices  10.8 us (14%)
  between operations  1.33 us (2%)
    all_to_all x1, blocking collectives, body(): returned = lax.all_to_all(returning, 'ctx', 0, 0, tiled=True)  21.1 us
    all_to_all x1, blocking collectives, body(): squares = lax.all_to_all(squares, 'head', 0, 0, tiled=True)  17.9 us
    pallas_call x5, Pallas kernels, call(): pl.pallas_call(kernel, name=name, out_shape=shapes, in_specs=specs, out_s...  15.1 us
    all_to_all x1, waiting for transfers between devices, body(): gathered = lax.all_to_all(outgoing, 'ctx', 0, 0, tiled=True)  12.9 us
    all_to_all x1, starting transfers between devices, body(): gathered = lax.all_to_all(outgoing, 'ctx', 0, 0, tiled=True)  10.8 us
  transfers between devices with their start and end apart: 1, of which 1 were waited for; matrix products, arithmetic and copies ran while one was open for 0% of the time, Pallas kernels for 9%

profile of v3, /device:TPU:6, one launch (start us, length us, event | category | flops | bytes accessed | tf_op | source)
XLA Modules:
  0.0 79.2 jit_solution(16655685019602428558)
XLA Ops:
  0.6 3.8 %summary.1 = (f32[64,21,1,128]{3,2,1,0:T(1,128)}, f32[64,8,128]{2,1,0:T(8,128)S(1)}, s32[1]{0:T(128)}) custom-call(s32[4]{0:T(128)} %lengths_in.3, f32[4,512]{1,0:T(4,128)} %bitcast.7, bf16[512,4,128]{2,1,0:T(4,128)(2,1)} %refs_2_.1, bf16[512,4,128]{2,1,0:T(4,128)(2,1)} %refs_3_.1, bf16[8,2,4,128]{3,2,1,0:T(4,128)(2,1)} %refs_5_.1), custom_call_target="tpu_custom_call" | custom-call | bytes 4194304 | tf_op jit(solution)/shard_map/summary/pallas_call | solution.py:542
  5.1 10.8 %all-to-all-start.1 = ((f32[64,21,1,128]{3,2,1,0:T(1,128)}), f32[64,21,1,128]{3,2,1,0:T(1,128)S(1)}, u32[]{:S(2)}, u32[]{:S(2)}) async-start(f32[64,21,1,128]{3,2,1,0:T(1,128)} %get-tuple-element.24), calls=%async_computation.1 | async-start | bytes 1376256 | tf_op jit(solution)/shard_map/all_to_all | solution.py:602
  16.0 7.0 %local.1 = (f32[4,512,128]{2,1,0:T(8,128)S(1)}, bf16[4,512,128]{2,1,0:T(8,128)(2,1)S(1)}, f32[512,8]{1,0:T(8,128)S(1)}, f32[8,8,128]{2,1,0:T(8,128)S(1)}, f32[8,...) custom-call(s32[4]{0:T(128)} %lengths_in.3, s32[4]{0:T(128)} %owner_in.1, s32[2]{0:T(128)} %row_lengths.1, ...), custom_call_target="tpu_custom_call" | custom-call | flops 2000000000 | bytes 4194304 | tf_op jit(solution)/shard_map/local/pallas_call | solution.py:542
  23.0 12.9 %all-to-all-done.1.got = f32[64,21,1,128]{3,2,1,0:T(1,128)S(1)} async-done(((f32[64,21,1,128]{3,2,1,0:T(1,128)}), f32[64,21,1,128]{3,2,1,0:T(1,128)S(1)}, u32[]{:S(2)}, u32[]{:S(2)}) %all-to-all-start.1) | async-done | bytes 688160 | tf_op jit(solution)/shard_map/all_to_all | solution.py:602
  35.9 2.1 %scan.1 = f32[64,12,1,128]{3,2,1,0:T(1,128)S(1)} custom-call(s32[4]{0:T(128)} %lengths_in.3, s32[4]{0:T(128)} %owner_in.1, f32[64,21,1,128]{3,2,1,0:T(1,128)S(1)} %all-to-all-done.1.got, f32[64,8,128]{2,1,0:T(8,128)S(1)} %get-tuple-element.40.second), custom_call_target="tpu_custom_call" | custom-call | bytes 4194304 | tf_op jit(solution)/shard_map/scan/pallas_call | solution.py:542
  38.0 21.1 %all_to_all.20.got = f32[64,12,1,128]{3,2,1,0:T(1,128)S(1)} all-to-all(f32[64,12,1,128]{3,2,1,0:T(1,128)S(1)} %scan.1), channel_id=1, replica_groups=mesh['ctx'=64,'head'=8] {'ctx'}, dimensions={0} | all-to-all | bytes 786432 | tf_op jit(solution)/shard_map/all_to_all | solution.py:658
  59.1 0.8 %mix.1 = (f32[4,512,128]{2,1,0:T(8,128)S(1)}, f32[8,8,128]{2,1,0:T(8,128)S(1)}, f32[8,1,640]{2,1,0:T(1,128)S(1)}) custom-call(f32[64,12,1,128]{3,2,1,0:T(1,128)S(1)} %all_to_all.20.got, f32[4,512,128]{2,1,0:T(8,128)S(1)} %get-tuple-element.29.intra, bf16[4,512,128]{2,1,0:T(8,128)(2,1)S(1)} %get-tuple-element.30.query, f32[512,8]{1,0:T(8,128)S(1)} %get-tuple-element.31.gate, ...), custom_call_target="tpu_custom_call" | custom-call | bytes 4194304 | tf_op jit(solution)/shard_map/mix/pallas_call | solution.py:542
  59.9 17.9 %all_to_all.21.got = f32[8,1,640]{2,1,0:T(1,128)S(1)} all-to-all(f32[8,1,640]{2,1,0:T(1,128)S(1)} %get-tuple-element.34), channel_id=1, replica_groups=mesh['ctx'=64,'head'=8] {'head'}, dimensions={0} | all-to-all | bytes 40960 | tf_op jit(solution)/shard_map/all_to_all | solution.py:670
  77.9 1.4 %norm.1 = (bf16[512,4,128]{2,1,0:T(4,128)(2,1)}, bf16[8,2,4,128]{3,2,1,0:T(4,128)(2,1)}) custom-call(f32[8,1,640]{2,1,0:T(1,128)S(1)} %all_to_all.21.got, f32[4,512,128]{2,1,0:T(8,128)S(1)} %get-tuple-element.35.mixed, f32[8,8,128]{2,1,0:T(8,128)S(1)} %get-tuple-element.36.reads), custom_call_target="tpu_custom_call" | custom-call | bytes 4194304 | tf_op jit(solution)/shard_map/norm/pallas_call | solution.py:542
  (1 shorter events, 0.0 us)
Async XLA Ops:
  5.1 30.7 %all-to-all-start.1 = ((f32[64,21,1,128]{3,2,1,0:T(1,128)}), f32[64,21,1,128]{3,2,1,0:T(1,128)S(1)}, u32[]{:S(2)}, u32[]{:S(2)}) async-start(f32[64,21,1,128]{3,2,1,0:T(1,128)} %get-tuple-element.24), calls=%async_computation.1 | async-start | bytes 1376256 | tf_op jit(solution)/shard_map/all_to_all | solution.py:602

commit v4 on v3

--- a/solution.py
+++ b/solution.py
@@ -15,9 +15,10 @@
 QUARTER = HD // 4
 ROW_END = 8
 ROW_QUERY = 16
-ROW_DECAY = 20
-ROWS_OUT = 21
-ROWS_BACK = 12
+ROW_DECAY = 18
+ROWS_OUT = 19
+ROWS_BACK = 10
+ROWS_SECOND = 10
 NT = (((1,), (1,)), ((), ()))
 TN = (((0,), (0,)), ((), ()))
 NN = (((1,), (0,)), ((), ()))
@@ -120,6 +121,13 @@
     return prompt, offset
 
 
+def row_taken(owner, row):
+    taken = jnp.bool_(False)
+    for p in range(owner.shape[0]):
+        taken = taken | (owner[p] == row)
+    return taken
+
+
 def block_shares(first, second, block):
     inside = (lax.rem(first, block) != 0) & (lax.rem(second, block) != 0)
     return inside & (first // block == second // block)
@@ -127,6 +135,7 @@
 
 def summary_kernel(
     lengths_in,
+    owner_in,
     decay,
     key,
     value,
@@ -139,6 +148,7 @@
     decay_buf,
     query_buf,
     lengths,
+    owner,
     sems,
 ):
     copies = [
@@ -151,17 +161,25 @@
         part = pl.ds(k * quarter, quarter)
         copies.append(pltpu.make_async_copy(key.at[part], key_buf.at[part], sems.at[2 + k]))
         copies.append(pltpu.make_async_copy(value.at[part], value_buf.at[part], sems.at[6 + k]))
-    bounds = pltpu.make_async_copy(lengths_in, lengths, sems.at[10])
-    bounds.start()
-    for copy in copies:
+    scalars = [
+        pltpu.make_async_copy(lengths_in, lengths, sems.at[10]),
+        pltpu.make_async_copy(owner_in, owner, sems.at[11]),
+    ]
+    for copy in scalars + copies:
         copy.start()
-    block_start = lax.axis_index("ctx") * block
-    bounds.wait()
+    device = lax.axis_index("ctx")
+    block_start = device * block
+    for copy in scalars:
+        copy.wait()
     _, ends = prompt_bounds(lengths)
     shared = jnp.bool_(False)
     for other in range(0, len(ends), 2):
         shared = shared | block_shares(ends[1], ends[other], block)
+    for p in range(len(ends)):
+        for other in range(p):
+            shared = shared | (owner[p] // 2 == owner[other] // 2)
     shared_out[0] = shared.astype(jnp.int32)
+    second_row = jnp.logical_not(row_taken(owner, device * 2))
     place = iota((1, block), 1)
     segment = segment_of(place + block_start, ends)
     last = scalar_segment(block_start + block - 1, ends)
@@ -206,14 +224,18 @@
             part = jnp.where(mine, read[low : low + pairs], 0.0)
             total = part if total is None else total + part
         spread.append(total)
-    spread = jnp.concatenate(spread, axis=0).reshape(2 * rows, heads, 4 * HD)
-    spread = jnp.swapaxes(spread, 0, 1)
     for h in range(heads):
+        first = jnp.concatenate([part[h : h + 1] for part in spread], axis=0)
+        other = jnp.concatenate([part[heads + h : heads + h + 1] for part in spread], axis=0)
+        chosen = jnp.where(second_row, other, first)
         for d in range(4):
-            piece = spread[h, :, d * HD : (d + 1) * HD]
             j = 16 * h + 4 * d
+            low = d * HD
             out[j : j + 4, ROW_QUERY:ROW_DECAY, 0, :] = jnp.broadcast_to(
-                piece[None], (4, 2 * rows, HD)
+                chosen[None, :, low : low + HD], (4, 2, HD)
+            )
+            second_out[j : j + 4, 8:ROWS_SECOND, 0, :] = jnp.broadcast_to(
+                other[None, :, low : low + HD], (4, 2, HD)
             )
 
     for copy in copies[2:]:
@@ -236,11 +258,11 @@
         for h in range(heads):
             left = two(keys[h].T.astype(f32) * weight_b[h : h + 1])
             product = mm(jnp.concatenate(left, axis=0), values[h])
-            second_out[16 * h : 16 * h + 16] = cut(product[:HD] + product[HD:])
+            second_out[16 * h : 16 * h + 16, 0:8, 0, :] = cut(product[:HD] + product[HD:])
 
     @pl.when(jnp.logical_not(both))
     def _():
-        second_out[...] = jnp.zeros(second_out.shape, f32)
+        second_out[:, 0:8, 0, :] = jnp.zeros((second_out.shape[0], 8, HD), f32)
 
 
 def local_kernel(lengths, owner, row_lengths, *refs):
@@ -327,10 +349,9 @@
     cum_col = cum_row.T
     causal = iota((steps, steps), 0) >= iota((steps, steps), 1)
     for r in range(rows_n):
-        owned = jnp.int32(0)
-        for p in range(len(ends)):
-            owned = owned + (owner[p] == device * rows_n + r).astype(jnp.int32)
-        owned = jnp.where(owned > 0, 1.0, 0.0)
+        taken = row_taken(owner, device * rows_n + r)
+        owned = jnp.where(taken, 1.0, 0.0)
+        late = jnp.where(taken & row_taken(owner, device * rows_n), r * 1.0, 0.0)
         for h in range(heads):
             n = r * heads + h
             cum = cum_col[:, n : n + 1]
@@ -345,7 +366,8 @@
             grown = jnp.exp(cum)
             read = (read[:, :HD] + read[:, HD:]) * grown
             base_out[n] = fresh + jnp.where(owned > 0.5, 0.0, read)
-            coef_out[n] = jnp.broadcast_to(grown * owned, (steps, HD))
+            coef_out[0, n] = jnp.broadcast_to(grown * (owned - late), (steps, HD))
+            coef_out[1, n] = jnp.broadcast_to(grown * late, (steps, HD))
 
     fresh_keys = jnp.swapaxes(new_keys[...].astype(f32), 0, 1)
     fresh_values = jnp.swapaxes(new_values[...].astype(f32), 0, 1)
@@ -374,7 +396,7 @@
 
 
 def scan_kernel(
-    block, lengths_in, owner_in, got, second, out, carried, lengths, owner, sems
+    block, lengths_in, owner_in, got, second, out, second_out, carried, lengths, owner, sems
 ):
     copies = [
         pltpu.make_async_copy(lengths_in, lengths, sems.at[0]),
@@ -424,10 +446,8 @@
         if i < ROWS_BACK - 8:
             out[:, 8 + i, 0, :] = jnp.zeros((blocks, HD), f32)
 
-    rows_n = (ROW_DECAY - ROW_QUERY) // 2
-    steps = 8
-    lane, step_at = iota((steps, HD), 1), iota((steps, HD), 0)
-    mine = lane // QUARTER == step_at % 4
+    second_out[...] = jnp.zeros(second_out.shape, f32)
+    mine = iota((HD, 1), 0) // QUARTER == iota((1, HD), 1) // QUARTER
     reads = []
     for p in range(len(ends)):
         index = ends[p] // block
@@ -446,28 +466,31 @@
         lead = leads * jnp.exp(jnp.where(partial, run, 0.0))
         rest = got[source, ROW_END : ROW_END + 8, 0, :]
         if p % 2:
-            rest = jnp.where(shared, second[source], rest)
+            rest = jnp.where(shared, second[source, 0:8, 0, :], rest)
         handed = carried[index] * lead + jnp.where(partial, rest, 0.0)
-        handed = [handed[:, g * QUARTER : (g + 1) * QUARTER] for g in range(4)]
-        high, low = two(jnp.concatenate(handed, axis=0))
-        both = jnp.concatenate([jnp.concatenate([high, low], axis=1)] * 4, axis=0)
-        place = owner[p] // rows_n
-        side = lax.rem(owner[p], rows_n)
+        rows = []
+        for g in range(4):
+            rows.append(jnp.concatenate([handed[:, g * QUARTER : (g + 1) * QUARTER]] * 4, axis=1))
+        rows = jnp.where(mine, jnp.concatenate(rows * 4, axis=0), 0.0)
+        place = owner[p] // 2
+        late = (lax.rem(owner[p], 2) == 1) & row_taken(owner, owner[p] - 1)
         query = jnp.where(
-            step_at < 4,
-            got[place, ROW_QUERY + side, :, :],
-            got[place, ROW_QUERY + rows_n + side, :, :],
+            late, second[place, 8:ROWS_SECOND, 0, :], got[place, ROW_QUERY:ROW_DECAY, 0, :]
         )
-        read = mm(jnp.where(mine, query, 0.0).astype(bf16), both)
-        read = read[:, :QUARTER] + read[:, QUARTER:]
-        reads.append((place, side, jnp.concatenate([read[:4], read[4:]] * 2, axis=1)))
-    for place, side, read in reads:
-        old = out[place, 8:ROWS_BACK, 0, :]
-        kept = lane[:4] // (2 * QUARTER) == side
-        out[place, 8:ROWS_BACK, 0, :] = jnp.where(kept, read, old)
-
-
-def mix_kernel(got, intra, query, gate, base, coef, mixed_out, reads_out, squares_out):
+        read = mm(query.astype(bf16), jnp.concatenate(two(rows), axis=1))
+        reads.append((place, late, read[:, :HD] + read[:, HD:]))
+    for place, late, read in reads:
+
+        @pl.when(late)
+        def _():
+            second_out[place, :, 0, :] = read
+
+        @pl.when(jnp.logical_not(late))
+        def _():
+            out[place, 8:ROWS_BACK, 0, :] = read
+
+
+def mix_kernel(got, second, intra, query, gate, base, coef, mixed_out, reads_out, squares_out):
     heads, block, _ = intra.shape
     total = None
     for h in range(heads):
@@ -482,20 +505,26 @@
     planes = squares_out.shape[0]
     squares_out[:, 0, :block] = (mm(ones, high, NT) + mm(ones, low, NT))[:planes]
 
+    def handed_reads(ref, low):
+        pieces = []
+        for e in range(4):
+            parts = []
+            for h in range(heads):
+                total = ref[16 * h + e, low : low + 2, 0, :]
+                for d in range(1, 4):
+                    total = total + ref[16 * h + 4 * d + e, low : low + 2, 0, :]
+                parts.append(total)
+            pieces.append(jnp.concatenate(parts, axis=0))
+        whole = jnp.swapaxes(jnp.stack(turn(*pieces), axis=0), 0, 1)
+        return whole.reshape(heads, 8, HD)
+
+    first, late = handed_reads(got, 8), handed_reads(second, 0)
     rows_n = base.shape[0] // heads
     squares = [None] * rows_n
     for h in range(heads):
-        pieces = []
-        for e in range(4):
-            total = got[16 * h + e, 8:ROWS_BACK, 0, :]
-            for d in range(1, 4):
-                total = total + got[16 * h + 4 * d + e, 8:ROWS_BACK, 0, :]
-            pieces.append(total)
-        pieces = turn(*pieces)
         for r in range(rows_n):
-            handed = jnp.concatenate(pieces[2 * r : 2 * r + 2], axis=0)
             n = r * heads + h
-            read = base[n] + coef[n] * handed
+            read = base[n] + coef[0, n] * first[h] + coef[1, n] * late[h]
             reads_out[n] = read
             squares[r] = read * read if squares[r] is None else squares[r] + read * read
     high, low = two(jnp.concatenate(squares, axis=0))
@@ -584,10 +613,10 @@
         "summary",
         [
             ((blocks, ROWS_OUT, 1, HD), f32),
-            ((blocks, 8, HD), f32),
+            ((blocks, ROWS_SECOND, 1, HD), f32),
             ((1,), jnp.int32),
         ],
-        [lengths],
+        [lengths, owner],
         [decay_rows, prefill_key, prefill_value, step_query],
         scratch=[
             pltpu.VMEM(prefill_key.shape, bf16),
@@ -595,17 +624,12 @@
             pltpu.VMEM(decay_rows.shape, f32),
             pltpu.VMEM(step_query.shape, bf16),
             pltpu.SMEM(lengths.shape, jnp.int32),
-            pltpu.SemaphoreType.DMA((11,)),
+            pltpu.SMEM(owner.shape, jnp.int32),
+            pltpu.SemaphoreType.DMA((12,)),
         ],
         space=pltpu.HBM,
     )
     gathered = lax.all_to_all(outgoing, "ctx", 0, 0, tiled=True)
-    second = lax.cond(
-        shared[0] > 0,
-        lambda x: lax.all_to_all(x, "ctx", 0, 0, tiled=True),
-        lambda x: x,
-        second,
-    )
     local_inputs = [
         decay_rows,
         prefill_query,
@@ -630,7 +654,7 @@
             ((heads, block, HD), bf16),
             ((block, 8), f32),
             ((pairs, steps, HD), f32),
-            ((pairs, steps, HD), f32),
+            ((2, pairs, steps, HD), f32),
             (soft_query.shape, bf16),
         ],
         [lengths, owner, row_lengths],
@@ -641,11 +665,18 @@
         space=pltpu.HBM,
         scalar_space=pltpu.SMEM,
     )
-    gathered, intra = lax.optimization_barrier((gathered, intra))
-    returning = call(
+    shared, intra = lax.optimization_barrier((shared, intra))
+    gathered, second = lax.optimization_barrier((gathered, second))
+    slow = shared[0] > 0
+
+    def exchange(x):
+        return lax.all_to_all(x, "ctx", 0, 0, tiled=True)
+
+    second = lax.cond(slow, exchange, lambda x: x, second)
+    returning, second = call(
         functools.partial(scan_kernel, block),
         "scan",
-        [((blocks, ROWS_BACK, 1, HD), f32)],
+        [((blocks, ROWS_BACK, 1, HD), f32), ((blocks, 2, 1, HD), f32)],
         [lengths, owner],
         [gathered, second],
         scratch=[
@@ -654,8 +685,9 @@
             pltpu.SMEM(owner.shape, jnp.int32),
             pltpu.SemaphoreType.DMA((2,)),
         ],
-    )[0]
+    )
     returned = lax.all_to_all(returning, "ctx", 0, 0, tiled=True)
+    second = lax.cond(slow, exchange, lambda x: x, second)
     mixed, reads, squares = call(
         mix_kernel,
         "mix",
@@ -665,7 +697,7 @@
             ((planes, 1, block + HD), f32),
         ],
         [],
-        [returned, intra, queries, gate, base, coef],
+        [returned, second, intra, queries, gate, base, coef],
     )
     squares = lax.all_to_all(squares, "head", 0, 0, tiled=True)
     prefill_out, decode_out = call(

time: 79.6 us -> 76.2 us (0.957)
  waiting for transfers between devices: 12.9 us -> 11 us
  blocking collectives: 39 us -> 37.6 us
    all_to_all x1, waiting for transfers between devices: 12.9 us -> 11 us  [body(): gathered = lax.all_to_all(outgoing, 'ctx', 0, 0, tiled=True)]
    all_to_all x1, blocking collectives: 21.1 us -> 19.7 us  [body(): returned = lax.all_to_all(returning, 'ctx', 0, 0, tiled=True)]
where the time goes in v4:
time: 76.2 us; the launch traced here: 75.9 us
  blocking collectives  37.6 us (49%)
  Pallas kernels  15.1 us (20%)
  waiting for transfers between devices  11 us (14%)
  starting transfers between devices  10.8 us (14%)
  between operations  1.33 us (2%)
    all_to_all x1, blocking collectives, body(): returned = lax.all_to_all(returning, 'ctx', 0, 0, tiled=True)  19.7 us
    all_to_all x1, blocking collectives, body(): squares = lax.all_to_all(squares, 'head', 0, 0, tiled=True)  17.9 us
    pallas_call x5, Pallas kernels, call(): pl.pallas_call(kernel, name=name, out_shape=shapes, in_specs=specs, out_s...  15.1 us
    all_to_all x1, waiting for transfers between devices, body(): gathered = lax.all_to_all(outgoing, 'ctx', 0, 0, tiled=True)  11 us
    all_to_all x1, starting transfers between devices, body(): gathered = lax.all_to_all(outgoing, 'ctx', 0, 0, tiled=True)  10.8 us
  transfers between devices with their start and end apart: 1, of which 1 were waited for; matrix products, arithmetic and copies ran while one was open for 0% of the time, Pallas kernels for 9%

profile of v4, /device:TPU:6, one launch (start us, length us, event | category | flops | bytes accessed | tf_op | source)
XLA Modules:
  0.0 75.9 jit_solution(11249818081111903747)
XLA Ops:
  0.6 4.0 %summary.1 = (f32[64,19,1,128]{3,2,1,0:T(1,128)}, f32[64,10,1,128]{3,2,1,0:T(1,128)S(1)}, s32[1]{0:T(128)}) custom-call(s32[4]{0:T(128)} %lengths_in.3, s32[4]{0:T(128)} %owner_in.3, f32[4,512]{1,0:T(4,128)} %bitcast.7, bf16[512,4,128]{2,1,0:T(4,128)(2,1)} %refs_2_.1, bf16[512,4,128]{2,1,0:T(4,128)(2,1)} %refs_3_.1, bf16[8,2,4,128]{3,2,1,0:T(4,128)(2,1)} %refs_5_.1), custom_call_target="tpu_custom_call" | custom-call | bytes 4194304 | tf_op jit(solution)/shard_map/summary/pallas_call | solution.py:571
  4.7 10.8 %all-to-all-start.2 = ((f32[64,19,1,128]{3,2,1,0:T(1,128)}), f32[64,19,1,128]{3,2,1,0:T(1,128)S(1)}, u32[]{:S(2)}, u32[]{:S(2)}) async-start(f32[64,19,1,128]{3,2,1,0:T(1,128)} %get-tuple-element.33), calls=%async_computation.2 | async-start | bytes 1245184 | tf_op jit(solution)/shard_map/all_to_all | solution.py:632
  15.5 7.0 %local.1 = (f32[4,512,128]{2,1,0:T(8,128)S(1)}, bf16[4,512,128]{2,1,0:T(8,128)(2,1)S(1)}, f32[512,8]{1,0:T(8,128)S(1)}, f32[8,8,128]{2,1,0:T(8,128)S(1)}, f32[2,...) custom-call(s32[4]{0:T(128)} %lengths_in.3, s32[4]{0:T(128)} %owner_in.3, s32[2]{0:T(128)} %row_lengths.1, ...), custom_call_target="tpu_custom_call" | custom-call | flops 2000000000 | bytes 4194304 | tf_op jit(solution)/shard_map/local/pallas_call | solution.py:571
  23.1 11.0 %all-to-all-done.2.got = f32[64,19,1,128]{3,2,1,0:T(1,128)S(1)} async-done(((f32[64,19,1,128]{3,2,1,0:T(1,128)}), f32[64,19,1,128]{3,2,1,0:T(1,128)S(1)}, u32[]{:S(2)}, u32[]{:S(2)}) %all-to-all-start.2) | async-done | bytes 622624 | tf_op jit(solution)/shard_map/all_to_all | solution.py:632
  34.1 1.9 %scan.1 = (f32[64,10,1,128]{3,2,1,0:T(1,128)S(1)}, f32[64,2,1,128]{3,2,1,0:T(1,128)S(1)}) custom-call(s32[4]{0:T(128)} %lengths_in.3, s32[4]{0:T(128)} %owner_in.3, f32[64,19,1,128]{3,2,1,0:T(1,128)S(1)} %all-to-all-done.2.got, f32[64,10,1,128]{3,2,1,0:T(1,128)S(1)} %get-tuple-element.53.second), custom_call_target="tpu_custom_call" | custom-call | bytes 4194304 | tf_op jit(solution)/shard_map/scan/pallas_call | solution.py:571
  36.0 19.7 %all_to_all.25.got = f32[64,10,1,128]{3,2,1,0:T(1,128)S(1)} all-to-all(f32[64,10,1,128]{3,2,1,0:T(1,128)S(1)} %get-tuple-element.40), channel_id=1, replica_groups=mesh['ctx'=64,'head'=8] {'ctx'}, dimensions={0} | all-to-all | bytes 655360 | tf_op jit(solution)/shard_map/all_to_all | solution.py:689
  55.8 0.8 %mix.1 = (f32[4,512,128]{2,1,0:T(8,128)S(1)}, f32[8,8,128]{2,1,0:T(8,128)S(1)}, f32[8,1,640]{2,1,0:T(1,128)S(1)}) custom-call(f32[64,10,1,128]{3,2,1,0:T(1,128)S(1)} %all_to_all.25.got, f32[64,2,1,128]{3,2,1,0:T(1,128)S(1)} %get-tuple-element.54.second, f32[4,512,128]{2,1,0:T(8,128)S(1)} %get-tuple-element.42.intra, ...), custom_call_target="tpu_custom_call" | custom-call | bytes 4194304 | tf_op jit(solution)/shard_map/mix/pallas_call | solution.py:571
  56.6 17.9 %all_to_all.26.got = f32[8,1,640]{2,1,0:T(1,128)S(1)} all-to-all(f32[8,1,640]{2,1,0:T(1,128)S(1)} %get-tuple-element.47), channel_id=1, replica_groups=mesh['ctx'=64,'head'=8] {'head'}, dimensions={0} | all-to-all | bytes 40960 | tf_op jit(solution)/shard_map/all_to_all | solution.py:702
  74.5 1.4 %norm.1 = (bf16[512,4,128]{2,1,0:T(4,128)(2,1)}, bf16[8,2,4,128]{3,2,1,0:T(4,128)(2,1)}) custom-call(f32[8,1,640]{2,1,0:T(1,128)S(1)} %all_to_all.26.got, f32[4,512,128]{2,1,0:T(8,128)S(1)} %get-tuple-element.48.mixed, f32[8,8,128]{2,1,0:T(8,128)S(1)} %get-tuple-element.49.reads), custom_call_target="tpu_custom_call" | custom-call | bytes 4194304 | tf_op jit(solution)/shard_map/norm/pallas_call | solution.py:571
  (2 shorter events, 0.0 us)
Async XLA Ops:
  4.7 29.5 %all-to-all-start.2 = ((f32[64,19,1,128]{3,2,1,0:T(1,128)}), f32[64,19,1,128]{3,2,1,0:T(1,128)S(1)}, u32[]{:S(2)}, u32[]{:S(2)}) async-start(f32[64,19,1,128]{3,2,1,0:T(1,128)} %get-tuple-element.33), calls=%async_computation.2 | async-start | bytes 1245184 | tf_op jit(solution)/shard_map/all_to_all | solution.py:632

commit v5 on v4

--- a/solution.py
+++ b/solution.py
@@ -140,9 +140,8 @@
     key,
     value,
     step_query,
-    out,
+    staged,
     second_out,
-    shared_out,
     key_buf,
     value_buf,
     decay_buf,
@@ -152,63 +151,23 @@
     sems,
 ):
     copies = [
-        pltpu.make_async_copy(decay, decay_buf, sems.at[0]),
-        pltpu.make_async_copy(step_query, query_buf, sems.at[1]),
+        pltpu.make_async_copy(lengths_in, lengths, sems.at[0]),
+        pltpu.make_async_copy(owner_in, owner, sems.at[1]),
+        pltpu.make_async_copy(step_query, query_buf, sems.at[2]),
+        pltpu.make_async_copy(decay, decay_buf, sems.at[3]),
     ]
     heads, block = decay_buf.shape
     quarter = block // 4
     for k in range(4):
         part = pl.ds(k * quarter, quarter)
-        copies.append(pltpu.make_async_copy(key.at[part], key_buf.at[part], sems.at[2 + k]))
-        copies.append(pltpu.make_async_copy(value.at[part], value_buf.at[part], sems.at[6 + k]))
-    scalars = [
-        pltpu.make_async_copy(lengths_in, lengths, sems.at[10]),
-        pltpu.make_async_copy(owner_in, owner, sems.at[11]),
-    ]
-    for copy in scalars + copies:
+        copies.append(pltpu.make_async_copy(key.at[part], key_buf.at[part], sems.at[4 + k]))
+        copies.append(pltpu.make_async_copy(value.at[part], value_buf.at[part], sems.at[8 + k]))
+    for copy in copies:
         copy.start()
     device = lax.axis_index("ctx")
     block_start = device * block
-    for copy in scalars:
-        copy.wait()
-    _, ends = prompt_bounds(lengths)
-    shared = jnp.bool_(False)
-    for other in range(0, len(ends), 2):
-        shared = shared | block_shares(ends[1], ends[other], block)
-    for p in range(len(ends)):
-        for other in range(p):
-            shared = shared | (owner[p] // 2 == owner[other] // 2)
-    shared_out[0] = shared.astype(jnp.int32)
-    second_row = jnp.logical_not(row_taken(owner, device * 2))
-    place = iota((1, block), 1)
-    segment = segment_of(place + block_start, ends)
-    last = scalar_segment(block_start + block - 1, ends)
-    prompt_a, offset_a = end_slot(0, ends, block_start, block)
-    prompt_b, offset_b = end_slot(1, ends, block_start, block)
-    both = (prompt_a >= 0) & (prompt_b >= 0)
-    prompt_a = jnp.where(prompt_a >= 0, prompt_a, prompt_b)
-    offset_a = jnp.where(offset_a >= 0, offset_a, offset_b)
-    copies[0].wait()
-    running = running_sums(decay_buf[...])
-
-    def weight(prompt, offset):
-        inside = segment == prompt
-        at = jnp.sum(jnp.where(place == offset, running, 0.0), axis=1, keepdims=True)
-        weight = jnp.where(inside, jnp.exp(jnp.where(inside, at - running, 0.0)), 0.0)
-        return weight, at
-
-    weight_last, _ = weight(last, jnp.int32(block - 1))
-    weight_a, at_a = weight(prompt_a, offset_a)
-    weight_b, at_b = weight(prompt_b, offset_b)
-    whole = jnp.sum(jnp.where(segment == last, decay_buf[...], 0.0), axis=1, keepdims=True)
-    lane, head = iota((heads, HD), 1), iota((heads, HD), 0)
-    totals = jnp.where(lane == head, whole, 0.0)
-    totals = jnp.where(lane == heads + head, at_a, totals)
-    totals = jnp.where(lane == 2 * heads + head, at_b, totals)
-    totals = jnp.sum(totals, axis=0, keepdims=True)
-    out[:, ROW_DECAY, 0, :] = jnp.broadcast_to(totals, (out.shape[0], HD))
-
-    copies[1].wait()
+
+    copies[2].wait()
     steps, rows = query_buf.shape[0], query_buf.shape[1]
     pairs = rows * heads
     flat = query_buf[...].astype(f32).reshape(steps * pairs, HD).astype(bf16)
@@ -224,21 +183,61 @@
             part = jnp.where(mine, read[low : low + pairs], 0.0)
             total = part if total is None else total + part
         spread.append(total)
+
+    copies[3].wait()
+    running = running_sums(decay_buf[...])
+
+    for copy in copies[:2]:
+        copy.wait()
+    _, ends = prompt_bounds(lengths)
+    place = iota((1, block), 1)
+    segment = segment_of(place + block_start, ends)
+    last = scalar_segment(block_start + block - 1, ends)
+    prompt_a, offset_a = end_slot(0, ends, block_start, block)
+    prompt_b, offset_b = end_slot(1, ends, block_start, block)
+    both = (prompt_a >= 0) & (prompt_b >= 0)
+    prompt_a = jnp.where(prompt_a >= 0, prompt_a, prompt_b)
+    offset_a = jnp.where(offset_a >= 0, offset_a, offset_b)
+
+    def weight(prompt, offset):
+        inside = segment == prompt
+        at = jnp.sum(jnp.where(place == offset, running, 0.0), axis=1, keepdims=True)
+        weight = jnp.where(inside, jnp.exp(jnp.where(inside, at - running, 0.0)), 0.0)
+        return weight, at
+
+    weight_last, _ = weight(last, jnp.int32(block - 1))
+    weight_a, at_a = weight(prompt_a, offset_a)
+    weight_b, at_b = weight(prompt_b, offset_b)
+    whole = jnp.sum(jnp.where(segment == last, decay_buf[...], 0.0), axis=1, keepdims=True)
+    lane, head = iota((heads, HD), 1), iota((heads, HD), 0)
+    totals = jnp.where(lane == head, whole, 0.0)
+    totals = jnp.where(lane == heads + head, at_a, totals)
+    totals = jnp.where(lane == 2 * heads + head, at_b, totals)
+    totals = jnp.sum(totals, axis=0, keepdims=True)
+    staged[:, ROW_DECAY, 0, :] = jnp.broadcast_to(totals, (staged.shape[0], HD))
+
+    first_taken = row_taken(owner, device * rows)
     for h in range(heads):
         first = jnp.concatenate([part[h : h + 1] for part in spread], axis=0)
         other = jnp.concatenate([part[heads + h : heads + h + 1] for part in spread], axis=0)
-        chosen = jnp.where(second_row, other, first)
+        chosen = jnp.where(first_taken, first, other)
         for d in range(4):
             j = 16 * h + 4 * d
-            low = d * HD
-            out[j : j + 4, ROW_QUERY:ROW_DECAY, 0, :] = jnp.broadcast_to(
-                chosen[None, :, low : low + HD], (4, 2, HD)
+            staged[j : j + 4, ROW_QUERY:ROW_DECAY, 0, :] = jnp.broadcast_to(
+                chosen[None, :, d * HD : (d + 1) * HD], (4, 2, HD)
             )
-            second_out[j : j + 4, 8:ROWS_SECOND, 0, :] = jnp.broadcast_to(
-                other[None, :, low : low + HD], (4, 2, HD)
-            )
-
-    for copy in copies[2:]:
+
+    @pl.when(first_taken & row_taken(owner, device * rows + 1))
+    def _():
+        for h in range(heads):
+            other = jnp.concatenate([part[heads + h : heads + h + 1] for part in spread], axis=0)
+            for d in range(4):
+                j = 16 * h + 4 * d
+                second_out[j : j + 4, 8:ROWS_SECOND, 0, :] = jnp.broadcast_to(
+                    other[None, :, d * HD : (d + 1) * HD], (4, 2, HD)
+                )
+
+    for copy in copies[4:]:
         copy.wait()
     keys = jnp.swapaxes(key_buf[...], 0, 1)
     values = jnp.swapaxes(value_buf[...], 0, 1)
@@ -251,7 +250,7 @@
         for k in range(2):
             low = 2 * k * HD
             state = product[low : low + HD] + product[low + HD : low + 2 * HD]
-            out[16 * h : 16 * h + 16, 8 * k : 8 * k + 8, 0, :] = cut(state)
+            staged[16 * h : 16 * h + 16, 8 * k : 8 * k + 8, 0, :] = cut(state)
 
     @pl.when(both)
     def _():
@@ -260,15 +259,11 @@
             product = mm(jnp.concatenate(left, axis=0), values[h])
             second_out[16 * h : 16 * h + 16, 0:8, 0, :] = cut(product[:HD] + product[HD:])
 
-    @pl.when(jnp.logical_not(both))
-    def _():
-        second_out[:, 0:8, 0, :] = jnp.zeros((second_out.shape[0], 8, HD), f32)
-
 
 def local_kernel(lengths, owner, row_lengths, *refs):
-    count = (len(refs) - 7) // 2
-    sources, outs = refs[:count], refs[count : count + 6]
-    buffers, sems = refs[count + 6 : -1], refs[-1]
+    count = (len(refs) - 9) // 2
+    sources, outs = refs[:count], refs[count : count + 8]
+    buffers, sems = refs[count + 8 : -1], refs[-1]
     copies = [
         pltpu.make_async_copy(source, buffer, sems.at[k])
         for k, (source, buffer) in enumerate(zip(sources, buffers))
@@ -293,11 +288,26 @@
         new_keys,
         new_values,
     ) = buffers
-    intra_out, query_out, gate_out, base_out, coef_out, soft_out = outs
+    intra_out, query_out, gate_out, base_out, coef_out, soft_out, linked_out, shared_out = outs
     block, heads, _ = query.shape
     device = lax.axis_index("ctx")
     block_start = device * block
-    _, ends = prompt_bounds(lengths)
+    starts, ends = prompt_bounds(lengths)
+    shared_end, shared_row = jnp.bool_(False), jnp.bool_(False)
+    for other in range(0, len(ends), 2):
+        shared_end = shared_end | block_shares(ends[1], ends[other], block)
+    for p in range(len(ends)):
+        for other in range(p):
+            shared_row = shared_row | (owner[p] // 2 == owner[other] // 2)
+    shared_out[0] = (shared_end | shared_row).astype(jnp.int32)
+    shared_out[1] = shared_row.astype(jnp.int32)
+    to, frm = iota(linked_out.shape, 0), iota(linked_out.shape, 1)
+    linked = frm < to
+    for start in starts:
+        restart = start // block
+        linked = linked & ~((restart > frm) & (restart < to))
+    linked_out[...] = linked.astype(f32)
+
     running = running_sums(log_decay[...])
     columns = jnp.concatenate([running, running], axis=0).T
     place_row = iota((1, block), 1) + block_start
@@ -396,7 +406,7 @@
 
 
 def scan_kernel(
-    block, lengths_in, owner_in, got, second, out, second_out, carried, lengths, owner, sems
+    block, lengths_in, owner_in, got, second, links, out, second_out, carried, lengths, owner, sems
 ):
     copies = [
         pltpu.make_async_copy(lengths_in, lengths, sems.at[0]),
@@ -427,14 +437,7 @@
         right.append(jnp.concatenate([high, low, high], axis=0))
     right = jnp.concatenate(right, axis=1)
 
-    for copy in copies:
-        copy.wait()
-    starts, ends = prompt_bounds(lengths)
-    to, frm = iota((padded, blocks), 0), iota((padded, blocks), 1)
-    linked = frm < to
-    for start in starts:
-        restart = start // block
-        linked = linked & ~((restart > frm) & (restart < to))
+    linked = links[...] > 0.5
     weight = jnp.where(linked, jnp.exp(jnp.where(linked, gap, 0.0)), 0.0)
     high, low = two(weight)
     weights = jnp.concatenate([high, high, low], axis=1)
@@ -447,7 +450,10 @@
             out[:, 8 + i, 0, :] = jnp.zeros((blocks, HD), f32)
 
     second_out[...] = jnp.zeros(second_out.shape, f32)
-    mine = iota((HD, 1), 0) // QUARTER == iota((1, HD), 1) // QUARTER
+    quarter_of = iota((1, HD), 1) // QUARTER
+    for copy in copies:
+        copy.wait()
+    starts, ends = prompt_bounds(lengths)
     reads = []
     for p in range(len(ends)):
         index = ends[p] // block
@@ -468,10 +474,12 @@
         if p % 2:
             rest = jnp.where(shared, second[source, 0:8, 0, :], rest)
         handed = carried[index] * lead + jnp.where(partial, rest, 0.0)
+        turned = [handed] + [pltpu.roll(handed, k * QUARTER, 1) for k in range(1, 4)]
         rows = []
-        for g in range(4):
-            rows.append(jnp.concatenate([handed[:, g * QUARTER : (g + 1) * QUARTER]] * 4, axis=1))
-        rows = jnp.where(mine, jnp.concatenate(rows * 4, axis=0), 0.0)
+        for k in range(4):
+            for g in range(4):
+                rows.append(jnp.where(quarter_of == k, turned[(k - g) % 4], 0.0))
+        rows = jnp.concatenate(rows, axis=0)
         place = owner[p] // 2
         late = (lax.rem(owner[p], 2) == 1) & row_taken(owner, owner[p] - 1)
         query = jnp.where(
@@ -561,6 +569,7 @@
     cost=0,
     space=pltpu.VMEM,
     scalar_space=pltpu.HBM,
+    first_out=pltpu.VMEM,
 ):
     scalars = [pltpu.with_memory_space_constraint(x, pltpu.HBM) for x in scalars]
     if space is pltpu.HBM:
@@ -574,8 +583,8 @@
         out_shape=shapes,
         in_specs=specs,
         out_specs=[
-            pl.BlockSpec(memory_space=pltpu.SMEM if dtype == jnp.int32 else pltpu.VMEM)
-            for _, dtype in outs
+            pl.BlockSpec(memory_space=pltpu.SMEM if dtype == jnp.int32 else space_k)
+            for (_, dtype), space_k in zip(outs, [first_out] + [pltpu.VMEM] * len(outs))
         ],
         scratch_shapes=list(scratch),
         compiler_params=pltpu.CompilerParams(vmem_limit_bytes=24 * 2**20),
@@ -608,13 +617,12 @@
     planes = lax.axis_size("head")
     pairs = rows_n * heads
     decay_rows = jnp.swapaxes(log_decay, 0, 1)
-    outgoing, second, shared = call(
+    outgoing, second = call(
         summary_kernel,
         "summary",
         [
             ((blocks, ROWS_OUT, 1, HD), f32),
             ((blocks, ROWS_SECOND, 1, HD), f32),
-            ((1,), jnp.int32),
         ],
         [lengths, owner],
         [decay_rows, prefill_key, prefill_value, step_query],
@@ -646,7 +654,7 @@
         new_keys.reshape(steps, rows_n, HD),
         new_values.reshape(steps, rows_n, HD),
     ]
-    intra, queries, gate, base, coef, soft_out = call(
+    intra, queries, gate, base, coef, soft_out, links, shared = call(
         local_kernel,
         "local",
         [
@@ -656,6 +664,8 @@
             ((pairs, steps, HD), f32),
             ((2, pairs, steps, HD), f32),
             (soft_query.shape, bf16),
+            ((blocks + 8, blocks), f32),
+            ((2,), jnp.int32),
         ],
         [lengths, owner, row_lengths],
         local_inputs,
@@ -667,18 +677,17 @@
     )
     shared, intra = lax.optimization_barrier((shared, intra))
     gathered, second = lax.optimization_barrier((gathered, second))
-    slow = shared[0] > 0
 
     def exchange(x):
         return lax.all_to_all(x, "ctx", 0, 0, tiled=True)
 
-    second = lax.cond(slow, exchange, lambda x: x, second)
+    second = lax.cond(shared[0] > 0, exchange, lambda x: x, second)
     returning, second = call(
         functools.partial(scan_kernel, block),
         "scan",
         [((blocks, ROWS_BACK, 1, HD), f32), ((blocks, 2, 1, HD), f32)],
         [lengths, owner],
-        [gathered, second],
+        [gathered, second, links],
         scratch=[
             pltpu.VMEM((blocks + 8, 8, HD), f32),
             pltpu.SMEM(lengths.shape, jnp.int32),
@@ -687,7 +696,7 @@
         ],
     )
     returned = lax.all_to_all(returning, "ctx", 0, 0, tiled=True)
-    second = lax.cond(slow, exchange, lambda x: x, second)
+    second = lax.cond(shared[1] > 0, exchange, lambda x: x, second)
     mixed, reads, squares = call(
         mix_kernel,
         "mix",

time: 76.2 us -> 75.7 us (level)
  waiting for transfers between devices: 11 us -> 9.73 us
    all_to_all x1, waiting for transfers between devices: 11 us -> 9.73 us  [body(): gathered = lax.all_to_all(outgoing, 'ctx', 0, 0, tiled=True)]
  transfers between devices with their start and end apart: 1 -> 1, of which waited for: 1 -> 1; matrix products, arithmetic and copies ran while one was open for 0% -> 1% of each run, Pallas kernels for 9% -> 9%
where the time goes in v5:
time: 75.7 us; the launch traced here: 75.3 us
  blocking collectives  37.7 us (50%)
  Pallas kernels  14.5 us (19%)
  starting transfers between devices  10.8 us (14%)
  waiting for transfers between devices  9.73 us (13%)
  between operations  1.98 us (3%)
    all_to_all x1, blocking collectives, body(): returned = lax.all_to_all(returning, 'ctx', 0, 0, tiled=True)  19.7 us
    all_to_all x1, blocking collectives, body(): squares = lax.all_to_all(squares, 'head', 0, 0, tiled=True)  17.9 us
    pallas_call x5, Pallas kernels, call(): pl.pallas_call(kernel, name=name, out_shape=shapes, in_specs=specs, out_s...  14.5 us
    all_to_all x1, starting transfers between devices, body(): gathered = lax.all_to_all(outgoing, 'ctx', 0, 0, tiled=True)  10.8 us
    all_to_all x1, waiting for transfers between devices, body(): gathered = lax.all_to_all(outgoing, 'ctx', 0, 0, tiled=True)  9.73 us
  transfers between devices with their start and end apart: 1, of which 1 were waited for; matrix products, arithmetic and copies ran while one was open for 1% of the time, Pallas kernels for 9%

profile of v5, /device:TPU:6, one launch (start us, length us, event | category | flops | bytes accessed | tf_op | source)
XLA Modules:
  0.0 75.3 jit_solution(18370984359213626249)
XLA Ops:
  0.6 3.8 %summary.1 = (f32[64,19,1,128]{3,2,1,0:T(1,128)}, f32[64,10,1,128]{3,2,1,0:T(1,128)S(1)}) custom-call(s32[4]{0:T(128)} %lengths_in.3, s32[4]{0:T(128)} %owner_in.3, f32[4,512]{1,0:T(4,128)} %bitcast.8, bf16[512,4,128]{2,1,0:T(4,128)(2,1)} %refs_2_.1, bf16[512,4,128]{2,1,0:T(4,128)(2,1)} %refs_3_.1, bf16[8,2,4,128]{3,2,1,0:T(4,128)(2,1)} %refs_5_.1), custom_call_target="tpu_custom_call" | custom-call | bytes 4194304 | tf_op jit(solution)/shard_map/summary/pallas_call | solution.py:580
  4.4 10.8 %all-to-all-start.2 = ((f32[64,19,1,128]{3,2,1,0:T(1,128)}), f32[64,19,1,128]{3,2,1,0:T(1,128)S(1)}, u32[]{:S(2)}, u32[]{:S(2)}) async-start(f32[64,19,1,128]{3,2,1,0:T(1,128)} %get-tuple-element.34), calls=%async_computation.2 | async-start | bytes 1245184 | tf_op jit(solution)/shard_map/all_to_all | solution.py:640
  15.2 7.0 %local.1 = (f32[4,512,128]{2,1,0:T(8,128)S(1)}, bf16[4,512,128]{2,1,0:T(8,128)(2,1)S(1)}, f32[512,8]{1,0:T(8,128)S(1)}, f32[8,8,128]{2,1,0:T(8,128)S(1)}, f32[2,...) custom-call(s32[4]{0:T(128)} %lengths_in.3, s32[4]{0:T(128)} %owner_in.3, ...), custom_call_target="tpu_custom_call" | custom-call | flops 2000000000 | bytes 4194304 | tf_op jit(solution)/shard_map/local/pallas_call | solution.py:580
  22.3 0.6 fusion
  24.2 9.7 %all-to-all-done.2.got = f32[64,19,1,128]{3,2,1,0:T(1,128)S(1)} async-done(((f32[64,19,1,128]{3,2,1,0:T(1,128)}), f32[64,19,1,128]{3,2,1,0:T(1,128)S(1)}, u32[]{:S(2)}, u32[]{:S(2)}) %all-to-all-start.2) | async-done | bytes 622624 | tf_op jit(solution)/shard_map/all_to_all | solution.py:640
  33.9 1.6 %scan.1 = (f32[64,10,1,128]{3,2,1,0:T(1,128)S(1)}, f32[64,2,1,128]{3,2,1,0:T(1,128)S(1)}) custom-call(s32[4]{0:T(128)} %lengths_in.3, s32[4]{0:T(128)} %owner_in.3, f32[64,19,1,128]{3,2,1,0:T(1,128)S(1)} %all-to-all-done.2.got, f32[64,10,1,128]{3,2,1,0:T(1,128)S(1)} %get-tuple-element.57.second, f32[72,64]{1,0:T(8,128)S(1)} %get-tuple-element.41.links), custom_call_target="tpu_custom_call" | custom-call | bytes 4194304 | tf_op jit(solution)/shard_map/scan/pallas_call | solution.py:580
  35.5 19.7 %all_to_all.25.got = f32[64,10,1,128]{3,2,1,0:T(1,128)S(1)} all-to-all(f32[64,10,1,128]{3,2,1,0:T(1,128)S(1)} %get-tuple-element.42), channel_id=1, replica_groups=mesh['ctx'=64,'head'=8] {'ctx'}, dimensions={0} | all-to-all | bytes 655360 | tf_op jit(solution)/shard_map/all_to_all | solution.py:698
  55.2 0.8 %mix.1 = (f32[4,512,128]{2,1,0:T(8,128)S(1)}, f32[8,8,128]{2,1,0:T(8,128)S(1)}, f32[8,1,640]{2,1,0:T(1,128)S(1)}) custom-call(f32[64,10,1,128]{3,2,1,0:T(1,128)S(1)} %all_to_all.25.got, f32[64,2,1,128]{3,2,1,0:T(1,128)S(1)} %get-tuple-element.58.second, f32[4,512,128]{2,1,0:T(8,128)S(1)} %get-tuple-element.44.intra, ...), custom_call_target="tpu_custom_call" | custom-call | bytes 4194304 | tf_op jit(solution)/shard_map/mix/pallas_call | solution.py:580
  56.0 17.9 %all_to_all.26.got = f32[8,1,640]{2,1,0:T(1,128)S(1)} all-to-all(f32[8,1,640]{2,1,0:T(1,128)S(1)} %get-tuple-element.49), channel_id=1, replica_groups=mesh['ctx'=64,'head'=8] {'head'}, dimensions={0} | all-to-all | bytes 40960 | tf_op jit(solution)/shard_map/all_to_all | solution.py:711
  73.9 1.4 %norm.1 = (bf16[512,4,128]{2,1,0:T(4,128)(2,1)}, bf16[8,2,4,128]{3,2,1,0:T(4,128)(2,1)}) custom-call(f32[8,1,640]{2,1,0:T(1,128)S(1)} %all_to_all.26.got, f32[4,512,128]{2,1,0:T(8,128)S(1)} %get-tuple-element.50.mixed, f32[8,8,128]{2,1,0:T(8,128)S(1)} %get-tuple-element.51.reads), custom_call_target="tpu_custom_call" | custom-call | bytes 4194304 | tf_op jit(solution)/shard_map/norm/pallas_call | solution.py:580
  (2 shorter events, 0.0 us)
Async XLA Ops:
  4.4 29.5 %all-to-all-start.2 = ((f32[64,19,1,128]{3,2,1,0:T(1,128)}), f32[64,19,1,128]{3,2,1,0:T(1,128)S(1)}, u32[]{:S(2)}, u32[]{:S(2)}) async-start(f32[64,19,1,128]{3,2,1,0:T(1,128)} %get-tuple-element.34), calls=%async_computation.2 | async-start | bytes 1245184 | tf_op jit(solution)/shard_map/all_to_all | solution.py:640

commit v6 on v5

--- a/solution.py
+++ b/solution.py
@@ -96,16 +96,15 @@
 def running_sums(decay):
     heads, block = decay.shape
     upto = (iota((HD, 1), 0) <= iota((1, HD), 1)).astype(f32).astype(bf16)
+    upto = jnp.concatenate([upto, jnp.ones((HD, HD), bf16)], axis=1)
     pieces = [decay[:, low : low + HD] for low in range(0, block, HD)]
     stacked = jnp.concatenate(pieces, axis=0)
     local = sum(mm(part, upto) for part in three(stacked))
     out, before = [], None
     for k in range(len(pieces)):
-        piece = local[k * heads : (k + 1) * heads]
-        if before is not None:
-            piece = piece + before
-        out.append(piece)
-        before = piece[:, HD - 1 : HD]
+        rows = slice(k * heads, (k + 1) * heads)
+        out.append(local[rows, :HD] if before is None else local[rows, :HD] + before)
+        before = local[rows, HD:] if before is None else before + local[rows, HD:]
     return jnp.concatenate(out, axis=1)
 
 
@@ -207,12 +206,10 @@
 
     weight_last, _ = weight(last, jnp.int32(block - 1))
     weight_a, at_a = weight(prompt_a, offset_a)
-    weight_b, at_b = weight(prompt_b, offset_b)
     whole = jnp.sum(jnp.where(segment == last, decay_buf[...], 0.0), axis=1, keepdims=True)
     lane, head = iota((heads, HD), 1), iota((heads, HD), 0)
     totals = jnp.where(lane == head, whole, 0.0)
     totals = jnp.where(lane == heads + head, at_a, totals)
-    totals = jnp.where(lane == 2 * heads + head, at_b, totals)
     totals = jnp.sum(totals, axis=0, keepdims=True)
     staged[:, ROW_DECAY, 0, :] = jnp.broadcast_to(totals, (staged.shape[0], HD))
 
@@ -254,6 +251,9 @@
 
     @pl.when(both)
     def _():
+        weight_b, at_b = weight(prompt_b, offset_b)
+        more = jnp.sum(jnp.where(lane == 2 * heads + head, at_b, 0.0), axis=0, keepdims=True)
+        staged[:, ROW_DECAY, 0, :] = jnp.broadcast_to(totals + more, (staged.shape[0], HD))
         for h in range(heads):
             left = two(keys[h].T.astype(f32) * weight_b[h : h + 1])
             product = mm(jnp.concatenate(left, axis=0), values[h])
@@ -541,14 +541,21 @@
     squares_out[:, 0, block:] = sums[:planes]
 
 
-def norm_kernel(count, got, mixed, reads, prefill_out, decode_out):
+def norm_kernel(count, got, mixed, reads, prefill_out, decode_out, staged, staged_reads, sems):
     heads, block, _ = mixed.shape
     parts = jnp.concatenate(three(got[:, 0, :]), axis=0)
     ones = jnp.ones((parts.shape[0], HD), bf16)
     total = mm(parts, ones, TN)
     scale = lax.rsqrt(total / count + eps)
-    scaled = jnp.stack([mixed[h] * scale[:block] for h in range(heads)], axis=0)
-    prefill_out[...] = jnp.swapaxes(scaled, 0, 1).astype(bf16)
+    sent = []
+    half = block // 2
+    for k in range(2):
+        part = pl.ds(k * half, half)
+        scaled = [mixed[h, part, :] * scale[k * half : (k + 1) * half] for h in range(heads)]
+        staged[part] = jnp.swapaxes(jnp.stack(scaled, axis=0), 0, 1).astype(bf16)
+        copy = pltpu.make_async_copy(staged.at[part], prefill_out.at[part], sems.at[k])
+        copy.start()
+        sent.append(copy)
     steps, rows_n = decode_out.shape[0], decode_out.shape[1]
     pieces = []
     for r in range(rows_n):
@@ -556,7 +563,12 @@
         for h in range(heads):
             pieces.append(reads[r * heads + h] * scale[low : low + steps])
     scaled = jnp.swapaxes(jnp.stack(pieces, axis=0), 0, 1)
-    decode_out[...] = scaled.reshape(decode_out.shape).astype(bf16)
+    staged_reads[...] = scaled.reshape(decode_out.shape).astype(bf16)
+    copy = pltpu.make_async_copy(staged_reads, decode_out, sems.at[2])
+    copy.start()
+    sent.append(copy)
+    for copy in sent:
+        copy.wait()
 
 
 def call(
@@ -569,7 +581,7 @@
     cost=0,
     space=pltpu.VMEM,
     scalar_space=pltpu.HBM,
-    first_out=pltpu.VMEM,
+    out_space=pltpu.VMEM,
 ):
     scalars = [pltpu.with_memory_space_constraint(x, pltpu.HBM) for x in scalars]
     if space is pltpu.HBM:
@@ -583,8 +595,8 @@
         out_shape=shapes,
         in_specs=specs,
         out_specs=[
-            pl.BlockSpec(memory_space=pltpu.SMEM if dtype == jnp.int32 else space_k)
-            for (_, dtype), space_k in zip(outs, [first_out] + [pltpu.VMEM] * len(outs))
+            pl.BlockSpec(memory_space=pltpu.SMEM if dtype == jnp.int32 else out_space)
+            for _, dtype in outs
         ],
         scratch_shapes=list(scratch),
         compiler_params=pltpu.CompilerParams(vmem_limit_bytes=24 * 2**20),
@@ -715,6 +727,12 @@
         [(prefill_query.shape, bf16), (step_query.shape, bf16)],
         [],
         [squares, mixed, reads],
+        scratch=[
+            pltpu.VMEM(prefill_query.shape, bf16),
+            pltpu.VMEM(step_query.shape, bf16),
+            pltpu.SemaphoreType.DMA((3,)),
+        ],
+        out_space=pltpu.HBM,
     )
     return (prefill_out, decode_out, soft_out)
 

time: 75.7 us -> 75.5 us (level)
  no operation moved by 1% of the time
where the time goes in v6:
time: 75.5 us; the launch traced here: 75.1 us
  blocking collectives  37.6 us (50%)
  Pallas kernels  14.3 us (19%)
  starting transfers between devices  10.8 us (14%)
  waiting for transfers between devices  9.81 us (13%)
  between operations  1.98 us (3%)
    all_to_all x1, blocking collectives, body(): returned = lax.all_to_all(returning, 'ctx', 0, 0, tiled=True)  19.7 us
    all_to_all x1, blocking collectives, body(): squares = lax.all_to_all(squares, 'head', 0, 0, tiled=True)  17.9 us
    pallas_call x5, Pallas kernels, call(): pl.pallas_call(kernel, name=name, out_shape=shapes, in_specs=specs, out_s...  14.3 us
    all_to_all x1, starting transfers between devices, body(): gathered = lax.all_to_all(outgoing, 'ctx', 0, 0, tiled=True)  10.8 us
    all_to_all x1, waiting for transfers between devices, body(): gathered = lax.all_to_all(outgoing, 'ctx', 0, 0, tiled=True)  9.81 us
  transfers between devices with their start and end apart: 1, of which 1 were waited for; matrix products, arithmetic and copies ran while one was open for 1% of the time, Pallas kernels for 9%

profile of v6, /device:TPU:6, one launch (start us, length us, event | category | flops | bytes accessed | tf_op | source)
XLA Modules:
  0.0 75.1 jit_solution(17318690012695371966)
XLA Ops:
  0.6 3.7 %summary.1 = (f32[64,19,1,128]{3,2,1,0:T(1,128)}, f32[64,10,1,128]{3,2,1,0:T(1,128)S(1)}) custom-call(s32[4]{0:T(128)} %lengths_in.3, s32[4]{0:T(128)} %owner_in.3, f32[4,512]{1,0:T(4,128)} %bitcast.8, bf16[512,4,128]{2,1,0:T(4,128)(2,1)} %refs_2_.1, bf16[512,4,128]{2,1,0:T(4,128)(2,1)} %refs_3_.1, bf16[8,2,4,128]{3,2,1,0:T(4,128)(2,1)} %refs_5_.1), custom_call_target="tpu_custom_call" | custom-call | bytes 4194304 | tf_op jit(solution)/shard_map/summary/pallas_call | solution.py:592
  4.3 10.8 %all-to-all-start.2 = ((f32[64,19,1,128]{3,2,1,0:T(1,128)}), f32[64,19,1,128]{3,2,1,0:T(1,128)S(1)}, u32[]{:S(2)}, u32[]{:S(2)}) async-start(f32[64,19,1,128]{3,2,1,0:T(1,128)} %get-tuple-element.34), calls=%async_computation.2 | async-start | bytes 1245184 | tf_op jit(solution)/shard_map/all_to_all | solution.py:652
  15.1 6.9 %local.1 = (f32[4,512,128]{2,1,0:T(8,128)S(1)}, bf16[4,512,128]{2,1,0:T(8,128)(2,1)S(1)}, f32[512,8]{1,0:T(8,128)S(1)}, f32[8,8,128]{2,1,0:T(8,128)S(1)}, f32[2,...) custom-call(s32[4]{0:T(128)} %lengths_in.3, s32[4]{0:T(128)} %owner_in.3, ...), custom_call_target="tpu_custom_call" | custom-call | flops 2000000000 | bytes 4194304 | tf_op jit(solution)/shard_map/local/pallas_call | solution.py:592
  22.1 0.6 fusion
  24.0 9.8 %all-to-all-done.2.got = f32[64,19,1,128]{3,2,1,0:T(1,128)S(1)} async-done(((f32[64,19,1,128]{3,2,1,0:T(1,128)}), f32[64,19,1,128]{3,2,1,0:T(1,128)S(1)}, u32[]{:S(2)}, u32[]{:S(2)}) %all-to-all-start.2) | async-done | bytes 622624 | tf_op jit(solution)/shard_map/all_to_all | solution.py:652
  33.8 1.6 %scan.1 = (f32[64,10,1,128]{3,2,1,0:T(1,128)S(1)}, f32[64,2,1,128]{3,2,1,0:T(1,128)S(1)}) custom-call(s32[4]{0:T(128)} %lengths_in.3, s32[4]{0:T(128)} %owner_in.3, f32[64,19,1,128]{3,2,1,0:T(1,128)S(1)} %all-to-all-done.2.got, f32[64,10,1,128]{3,2,1,0:T(1,128)S(1)} %get-tuple-element.57.second, f32[72,64]{1,0:T(8,128)S(1)} %get-tuple-element.41.links), custom_call_target="tpu_custom_call" | custom-call | bytes 4194304 | tf_op jit(solution)/shard_map/scan/pallas_call | solution.py:592
  35.4 19.7 %all_to_all.25.got = f32[64,10,1,128]{3,2,1,0:T(1,128)S(1)} all-to-all(f32[64,10,1,128]{3,2,1,0:T(1,128)S(1)} %get-tuple-element.42), channel_id=1, replica_groups=mesh['ctx'=64,'head'=8] {'ctx'}, dimensions={0} | all-to-all | bytes 655360 | tf_op jit(solution)/shard_map/all_to_all | solution.py:710
  55.1 0.8 %mix.1 = (f32[4,512,128]{2,1,0:T(8,128)S(1)}, f32[8,8,128]{2,1,0:T(8,128)S(1)}, f32[8,1,640]{2,1,0:T(1,128)S(1)}) custom-call(f32[64,10,1,128]{3,2,1,0:T(1,128)S(1)} %all_to_all.25.got, f32[64,2,1,128]{3,2,1,0:T(1,128)S(1)} %get-tuple-element.58.second, f32[4,512,128]{2,1,0:T(8,128)S(1)} %get-tuple-element.44.intra, ...), custom_call_target="tpu_custom_call" | custom-call | bytes 4194304 | tf_op jit(solution)/shard_map/mix/pallas_call | solution.py:592
  55.9 17.9 %all_to_all.26.got = f32[8,1,640]{2,1,0:T(1,128)S(1)} all-to-all(f32[8,1,640]{2,1,0:T(1,128)S(1)} %get-tuple-element.49), channel_id=1, replica_groups=mesh['ctx'=64,'head'=8] {'head'}, dimensions={0} | all-to-all | bytes 40960 | tf_op jit(solution)/shard_map/all_to_all | solution.py:723
  73.8 1.3 %norm.1 = (bf16[512,4,128]{2,1,0:T(4,128)(2,1)}, bf16[8,2,4,128]{3,2,1,0:T(4,128)(2,1)}) custom-call(f32[8,1,640]{2,1,0:T(1,128)S(1)} %all_to_all.26.got, f32[4,512,128]{2,1,0:T(8,128)S(1)} %get-tuple-element.50.mixed, f32[8,8,128]{2,1,0:T(8,128)S(1)} %get-tuple-element.51.reads), custom_call_target="tpu_custom_call" | custom-call | bytes 4194304 | tf_op jit(solution)/shard_map/norm/pallas_call | solution.py:592
  (2 shorter events, 0.0 us)
Async XLA Ops:
  4.3 29.5 %all-to-all-start.2 = ((f32[64,19,1,128]{3,2,1,0:T(1,128)}), f32[64,19,1,128]{3,2,1,0:T(1,128)S(1)}, u32[]{:S(2)}, u32[]{:S(2)}) async-start(f32[64,19,1,128]{3,2,1,0:T(1,128)} %get-tuple-element.34), calls=%async_computation.2 | async-start | bytes 1245184 | tf_op jit(solution)/shard_map/all_to_all | solution.py:652

commit v7 on v6

--- a/solution.py
+++ b/solution.py
@@ -446,10 +446,7 @@
         state = product[:, i * HD : (i + 1) * HD]
         carried[:, i, :] = state
         out[:, i, 0, :] = state[:blocks]
-        if i < ROWS_BACK - 8:
-            out[:, 8 + i, 0, :] = jnp.zeros((blocks, HD), f32)
-
-    second_out[...] = jnp.zeros(second_out.shape, f32)
+
     quarter_of = iota((1, HD), 1) // QUARTER
     for copy in copies:
         copy.wait()
@@ -532,7 +529,8 @@
     for h in range(heads):
         for r in range(rows_n):
             n = r * heads + h
-            read = base[n] + coef[0, n] * first[h] + coef[1, n] * late[h]
+            read = base[n] + jnp.where(coef[0, n] > 0, coef[0, n] * first[h], 0.0)
+            read = read + jnp.where(coef[1, n] > 0, coef[1, n] * late[h], 0.0)
             reads_out[n] = read
             squares[r] = read * read if squares[r] is None else squares[r] + read * read
     high, low = two(jnp.concatenate(squares, axis=0))

time: 75.5 us -> 75.5 us (level)
  no operation moved by 1% of the time
where the time goes in v7:
time: 75.5 us; the launch traced here: 75.1 us
  blocking collectives  37.6 us (50%)
  Pallas kernels  14.3 us (19%)
  starting transfers between devices  10.8 us (14%)
  waiting for transfers between devices  9.81 us (13%)
  between operations  1.98 us (3%)
    all_to_all x1, blocking collectives, body(): returned = lax.all_to_all(returning, 'ctx', 0, 0, tiled=True)  19.7 us
    all_to_all x1, blocking collectives, body(): squares = lax.all_to_all(squares, 'head', 0, 0, tiled=True)  17.9 us
    pallas_call x5, Pallas kernels, call(): pl.pallas_call(kernel, name=name, out_shape=shapes, in_specs=specs, out_s...  14.3 us
    all_to_all x1, starting transfers between devices, body(): gathered = lax.all_to_all(outgoing, 'ctx', 0, 0, tiled=True)  10.8 us
    all_to_all x1, waiting for transfers between devices, body(): gathered = lax.all_to_all(outgoing, 'ctx', 0, 0, tiled=True)  9.81 us
  transfers between devices with their start and end apart: 1, of which 1 were waited for; matrix products, arithmetic and copies ran while one was open for 1% of the time, Pallas kernels for 9%

profile of v7, /device:TPU:6, one launch (start us, length us, event | category | flops | bytes accessed | tf_op | source)
XLA Modules:
  0.0 75.1 jit_solution(2693601699006334692)
XLA Ops:
  0.6 3.7 %summary.1 = (f32[64,19,1,128]{3,2,1,0:T(1,128)}, f32[64,10,1,128]{3,2,1,0:T(1,128)S(1)}) custom-call(s32[4]{0:T(128)} %lengths_in.3, s32[4]{0:T(128)} %owner_in.3, f32[4,512]{1,0:T(4,128)} %bitcast.8, bf16[512,4,128]{2,1,0:T(4,128)(2,1)} %refs_2_.1, bf16[512,4,128]{2,1,0:T(4,128)(2,1)} %refs_3_.1, bf16[8,2,4,128]{3,2,1,0:T(4,128)(2,1)} %refs_5_.1), custom_call_target="tpu_custom_call" | custom-call | bytes 4194304 | tf_op jit(solution)/shard_map/summary/pallas_call | solution.py:590
  4.3 10.8 %all-to-all-start.2 = ((f32[64,19,1,128]{3,2,1,0:T(1,128)}), f32[64,19,1,128]{3,2,1,0:T(1,128)S(1)}, u32[]{:S(2)}, u32[]{:S(2)}) async-start(f32[64,19,1,128]{3,2,1,0:T(1,128)} %get-tuple-element.34), calls=%async_computation.2 | async-start | bytes 1245184 | tf_op jit(solution)/shard_map/all_to_all | solution.py:650
  15.1 6.9 %local.1 = (f32[4,512,128]{2,1,0:T(8,128)S(1)}, bf16[4,512,128]{2,1,0:T(8,128)(2,1)S(1)}, f32[512,8]{1,0:T(8,128)S(1)}, f32[8,8,128]{2,1,0:T(8,128)S(1)}, f32[2,...) custom-call(s32[4]{0:T(128)} %lengths_in.3, s32[4]{0:T(128)} %owner_in.3, ...), custom_call_target="tpu_custom_call" | custom-call | flops 2000000000 | bytes 4194304 | tf_op jit(solution)/shard_map/local/pallas_call | solution.py:590
  22.1 0.6 fusion
  24.0 9.8 %all-to-all-done.2.got = f32[64,19,1,128]{3,2,1,0:T(1,128)S(1)} async-done(((f32[64,19,1,128]{3,2,1,0:T(1,128)}), f32[64,19,1,128]{3,2,1,0:T(1,128)S(1)}, u32[]{:S(2)}, u32[]{:S(2)}) %all-to-all-start.2) | async-done | bytes 622624 | tf_op jit(solution)/shard_map/all_to_all | solution.py:650
  33.8 1.6 %scan.1 = (f32[64,10,1,128]{3,2,1,0:T(1,128)S(1)}, f32[64,2,1,128]{3,2,1,0:T(1,128)S(1)}) custom-call(s32[4]{0:T(128)} %lengths_in.3, s32[4]{0:T(128)} %owner_in.3, f32[64,19,1,128]{3,2,1,0:T(1,128)S(1)} %all-to-all-done.2.got, f32[64,10,1,128]{3,2,1,0:T(1,128)S(1)} %get-tuple-element.57.second, f32[72,64]{1,0:T(8,128)S(1)} %get-tuple-element.41.links), custom_call_target="tpu_custom_call" | custom-call | bytes 4194304 | tf_op jit(solution)/shard_map/scan/pallas_call | solution.py:590
  35.4 19.7 %all_to_all.25.got = f32[64,10,1,128]{3,2,1,0:T(1,128)S(1)} all-to-all(f32[64,10,1,128]{3,2,1,0:T(1,128)S(1)} %get-tuple-element.42), channel_id=1, replica_groups=mesh['ctx'=64,'head'=8] {'ctx'}, dimensions={0} | all-to-all | bytes 655360 | tf_op jit(solution)/shard_map/all_to_all | solution.py:708
  55.1 0.8 %mix.1 = (f32[4,512,128]{2,1,0:T(8,128)S(1)}, f32[8,8,128]{2,1,0:T(8,128)S(1)}, f32[8,1,640]{2,1,0:T(1,128)S(1)}) custom-call(f32[64,10,1,128]{3,2,1,0:T(1,128)S(1)} %all_to_all.25.got, f32[64,2,1,128]{3,2,1,0:T(1,128)S(1)} %get-tuple-element.58.second, f32[4,512,128]{2,1,0:T(8,128)S(1)} %get-tuple-element.44.intra, ...), custom_call_target="tpu_custom_call" | custom-call | bytes 4194304 | tf_op jit(solution)/shard_map/mix/pallas_call | solution.py:590
  55.9 17.9 %all_to_all.26.got = f32[8,1,640]{2,1,0:T(1,128)S(1)} all-to-all(f32[8,1,640]{2,1,0:T(1,128)S(1)} %get-tuple-element.49), channel_id=1, replica_groups=mesh['ctx'=64,'head'=8] {'head'}, dimensions={0} | all-to-all | bytes 40960 | tf_op jit(solution)/shard_map/all_to_all | solution.py:721
  73.8 1.3 %norm.1 = (bf16[512,4,128]{2,1,0:T(4,128)(2,1)}, bf16[8,2,4,128]{3,2,1,0:T(4,128)(2,1)}) custom-call(f32[8,1,640]{2,1,0:T(1,128)S(1)} %all_to_all.26.got, f32[4,512,128]{2,1,0:T(8,128)S(1)} %get-tuple-element.50.mixed, f32[8,8,128]{2,1,0:T(8,128)S(1)} %get-tuple-element.51.reads), custom_call_target="tpu_custom_call" | custom-call | bytes 4194304 | tf_op jit(solution)/shard_map/norm/pallas_call | solution.py:590
  (2 shorter events, 0.0 us)
Async XLA Ops:
  4.3 29.5 %all-to-all-start.2 = ((f32[64,19,1,128]{3,2,1,0:T(1,128)}), f32[64,19,1,128]{3,2,1,0:T(1,128)S(1)}, u32[]{:S(2)}, u32[]{:S(2)}) async-start(f32[64,19,1,128]{3,2,1,0:T(1,128)} %get-tuple-element.34), calls=%async_computation.2 | async-start | bytes 1245184 | tf_op jit(solution)/shard_map/all_to_all | solution.py:650
